TPU v7x, 512 devices: a whole 4x4x16 slice. The times are simulated.
512 devices in a mesh: dp: 128 (over z_lo, x, y), mp: 4 (over z_hi, core).
Axes of the slice: x: 4, y: 4, z: 16 (z_hi: 2, z_lo: 8; z = z_hi * 8 + z_lo), core: 2. Of those that a mesh axis runs over, the one named last changes fastest.
Arguments:
- acts: bfloat16 [65536, 4608], P('dp', 'mp'), may hold values from -6 to 6
- cotangent: bfloat16 [65536, 2048], P('dp', 'mp'), may hold values from -6 to 6
- lengths: int32 [128, 8], P('dp'), may hold values from 1 to 64, as said below
- policy: int32 [128, 8], P('dp'), may hold values from 0 to 7
- advantages: float32 [128, 8], P('dp'), may hold values from -4 to 4
- sampler_log_prob: float32 [65536], P('dp'), may hold values from -4 to -0.5
- current_log_prob: float32 [65536], P('dp'), may hold values from -4 to -0.5
- down_factors: bfloat16 [4608, 512], P('mp'), may hold values from -0.09375 to 0.09375
- up_factors: bfloat16 [512, 2048], P(None, 'mp'), may hold values from -0.125 to 0.125
Outputs:
- grad_a: float32 [512, 4608], P('dp', 'mp')
- grad_b: float32 [512, 2048], P('dp', 'mp')
Inputs may be any that keep to these rules, and one draw needn't show every extreme that they name: `lengths`: each row sums to 512 or less, some row to exactly 512; the largest entry is exactly 64.
All inputs are finite; a program needn't handle non-finite values.
Results may differ from a plain program's by a relative error of at most 0.0005.
Values may be sent and summed in bfloat16 or wider, within the bound.
No kernel may reach another device: no remote copies, remote signals or barrier semaphores. Data moves between devices by JAX's collectives and lax.ppermute only.
A program may use at most 64 MiB of HBM per device.

v0:
```python
import jax
import jax.numpy as jnp
from jax import lax
from jax.sharding import PartitionSpec as P

ADAPTER_RANK = 64


ADAPTER_SCALE = 2.0
CLIP_LOW = 0.8
CLIP_HIGH = 1.28


def token_meta(
    seq_lengths, seq_policy, seq_advantages, sampler_log_prob, current_log_prob, capacity
):
    seq_count = seq_lengths.shape[0]
    bounds = jnp.cumsum(seq_lengths)
    position = jnp.arange(capacity, dtype=jnp.int32)
    seq_of = jnp.sum((position[:, None] >= bounds[None, :]).astype(jnp.int32), axis=1)
    policy_member = seq_of[:, None] == jnp.arange(seq_count, dtype=jnp.int32)[None, :]
    sequence_totals = seq_advantages / seq_lengths.astype(jnp.float32)
    probability_ratios = jnp.clip(jnp.exp(current_log_prob - sampler_log_prob), CLIP_LOW, CLIP_HIGH)
    frozen_weight = (
        ADAPTER_SCALE
        * jnp.sum(jnp.where(policy_member, sequence_totals[None, :], jnp.float32(0.0)), axis=1)
        * probability_ratios
    )
    token_policy = jnp.sum(policy_member.astype(jnp.int32) * seq_policy[None, :], axis=1)
    return (frozen_weight, token_policy, bounds)


def shards(
    acts,
    cotangent,
    lengths,
    policy,
    advantages,
    sampler_log_prob,
    current_log_prob,
    down_factors,
    up_factors,
):
    full_rows = acts.shape[0]
    number_policies = down_factors.shape[1] // ADAPTER_RANK
    frozen_weight, token_policy, bounds = token_meta(
        lengths[0], policy[0], advantages[0], sampler_log_prob, current_log_prob, full_rows
    )
    activation_rows, cotangent_rows, rows_weight, rows_policy = (
        acts,
        cotangent,
        frozen_weight,
        token_policy,
    )
    capacity = activation_rows.shape[0]
    owners = (rows_policy[:, None] == jnp.arange(number_policies, dtype=jnp.int32)[None, :]).astype(
        jnp.float32
    )
    spread = jnp.repeat(owners, ADAPTER_RANK, axis=1)
    reduced_input = jnp.dot(activation_rows, down_factors, preferred_element_type=jnp.float32)
    reduced_output = lax.dot_general(
        cotangent_rows, up_factors, (((1,), (1,)), ((), ())), preferred_element_type=jnp.float32
    )

    def select_own(full):
        return jnp.sum(
            full.reshape(capacity, number_policies, ADAPTER_RANK) * owners[:, :, None], axis=1
        )

    summed_in, summed_out = lax.psum((reduced_input, reduced_output), "mp")
    in_own = select_own(summed_in)
    out_own = select_own(summed_out)
    hidden_w = rows_weight[:, None] * in_own
    grad_w = rows_weight[:, None] * out_own
    hidden_wide = jnp.tile(hidden_w, (1, number_policies)) * spread
    grad_wide = jnp.tile(grad_w, (1, number_policies)) * spread
    acts_wide = activation_rows.astype(jnp.float32)
    cot_wide = cotangent_rows.astype(jnp.float32)
    columns = grad_wide
    grad_a = lax.psum_scatter(
        lax.dot_general(
            columns,
            acts_wide,
            (((0,), (0,)), ((), ())),
            precision=lax.Precision.HIGHEST,
            preferred_element_type=jnp.float32,
        ),
        "dp",
        scatter_dimension=0,
        tiled=True,
    )
    columns = hidden_wide
    grad_b = lax.psum_scatter(
        lax.dot_general(
            columns,
            cot_wide,
            (((0,), (0,)), ((), ())),
            precision=lax.Precision.HIGHEST,
            preferred_element_type=jnp.float32,
        ),
        "dp",
        scatter_dimension=0,
        tiled=True,
    )
    return (grad_a, grad_b)


def solution(mesh):
    return jax.shard_map(
        shards,
        mesh=mesh,
        in_specs=(
            P("dp", "mp"),
            P("dp", "mp"),
            P("dp", None),
            P("dp", None),
            P("dp", None),
            P("dp"),
            P("dp"),
            P("mp", None),
            P(None, "mp"),
        ),
        out_specs=(P("dp", "mp"), P("dp", "mp")),
        check_vma=False,
    )
```

profile of v0, /device:TPU:0, one launch (start us, length us, event | category | flops | bytes accessed | tf_op | source)
XLA Modules:
  0.0 2173.4 jit_solution(4517532571196594390)
XLA Ops:
  7.2 0.0 copy-start
  7.2 0.0 copy-start.5
  7.2 0.0 all-reduce.9.cloned.1.call-start
  7.2 2.8 fusion.2
  10.0 0.0 copy-done
  10.0 0.0 copy-done.5
  10.0 1.9 fusion.4
  11.9 0.0 copy-start.6
  11.9 0.0 copy-start.4
  11.9 0.0 copy-start.7
  11.9 0.0 copy-start.2
  11.9 0.0 copy-start.3
  11.9 0.0 all-reduce.9.cloned.1.call-update
  12.0 0.0 all-reduce.7.cloned.1.call-start
  12.0 0.6 copy-done.6
  12.6 0.2 reduce-window.8
  12.8 0.1 convert_reduce_fusion
  12.8 0.0 copy-done.4
  12.8 0.1 select_reduce_fusion
  12.9 0.0 copy-done.7
  12.9 0.1 select_reduce_fusion.1
  13.0 0.0 copy-done.2
  13.0 0.0 copy-done.3
  13.1 182.8 %all-reduce.9.cloned.1.call-done = (f32[512,8,64]{0,2,1:T(8,128)}, f32[512,8,64]{0,2,1:T(8,128)}) async-done(((f32[512,8,64]{0,2,1:T(8,128)}, f32[512,8,64]{0,2,1:T(8,128)}), (f32[512,8,64]{0,2,1:T(8,128)}, f32[512,8,64]{0,2,1:T(8,128)})) %all-reduce.9.cloned.1.call-update) | async-done | bytes 2097168 | tf_op jit(solution)/shard_map/psum | solution.py:70
  195.9 1.8 multiply_reduce_fusion
  197.8 0.3 broadcast_multiply_fusion
  198.0 0.0 copy-start.1
  198.0 3.6 fusion.3
  201.7 0.0 copy-done.1
  201.7 2.0 fusion.5
  203.7 0.0 all-reduce.7.cloned.1.call-update
  203.7 1.3 dynamic-slice
  205.6 1958.3 %all-reduce.7.cloned.1.call-done = (f32[512,1152]{1,0:T(8,128)}, f32[512,512]{1,0:T(8,128)}) async-done(((f32[512,1152]{1,0:T(8,128)}, f32[512,512]{1,0:T(8,128)}), (f32[512,1152]{1,0:T(8,128)}, f32[512,512]{1,0:T(8,128)})) %all-reduce.7.cloned.1.call-update) | async-done | bytes 3407888
  2163.9 1.4 constant_dynamic-slice_fusion.1
  2165.3 1.3 constant_dynamic-slice_fusion
  (4 shorter events, 0.0 us)
Async XLA Ops:
  7.2 2.9 copy-start
  7.2 2.9 copy-start.5
  7.2 188.7 %all-reduce.9.cloned.1.call-start = ((), (), s32[]{:S(2)}) async-start(), calls=%async_computation.1 | async-start | bytes 4194304 | tf_op jit(solution)/shard_map/psum | solution.py:70
  11.9 0.7 copy-start.6
  11.9 0.9 copy-start.4
  11.9 1.0 copy-start.7
  11.9 1.1 copy-start.2
  11.9 1.1 copy-start.3
  12.0 2151.9 %all-reduce.7.cloned.1.call-start = ((), (), s32[]{:S(2)}) async-start(), calls=%async_computation | async-start | bytes 6815744
  198.0 3.7 copy-start.1
Sparse Core Ops, SparseCore 0:
  12.1 183.7 all-reduce.8
  203.8 1960.0 all-reduce.6
where the time goes:
time: 2170 us
  waiting for transfers between devices  2140 us (99%)
    unnamed x3, waiting for transfers between devices  1960 us
    psum x1, waiting for transfers between devices, shards(): summed_in, summed_out = lax.psum((reduced_input, reduced_output), 'mp')  183 us
  transfers between devices with their start and end apart: 2, of which 2 were waited for; matrix products, arithmetic and copies ran while one was open for 0% of the time, Pallas kernels for 0%

commit v1 on v0

v1 whole, which is shorter than its diff:
```python
import functools

import jax
import jax.numpy as jnp
import numpy as np
from jax import lax
from jax.experimental import pallas as pl
from jax.experimental.pallas import tpu as pltpu
from jax.sharding import PartitionSpec as P

RANK = 64
POLICIES = 8
SEQS = 8
ADAPTER_SCALE = 2.0
CLIP_LOW = 0.8
CLIP_HIGH = 1.28
TINY = 1e-30
TOP = 32767.0
F32, BF16, I16, I32 = jnp.float32, jnp.bfloat16, jnp.int16, jnp.int32
BOTH = ("dp", "mp")
VMEM = pl.BlockSpec(memory_space=pltpu.VMEM)
SMEM = pl.BlockSpec(memory_space=pltpu.SMEM)


def code_of(largest):
    return jnp.ceil(jnp.log2(jnp.maximum(largest, TINY)) * 256.0) + 1.0


def scale_of(code):
    return jnp.exp2(code * (1.0 / 256.0))


def to_i16(values):
    return jnp.clip(jnp.round(values), -TOP, TOP).astype(I32).astype(I16)


def from_i16(values):
    return values.astype(I32).astype(F32)


def starts_of(lengths_ref):
    bounds = [jnp.int32(0)]
    for s in range(SEQS):
        bounds.append(bounds[-1] + lengths_ref[0, s])
    return bounds


def low_kernel(
    lengths_ref, policy_ref, adv_ref, old_ref, new_ref, acts_ref, cot_ref, down_ref, up_ref, keep_ref, send_ref, x_ref
):
    tokens = acts_ref.shape[0]
    half = tokens // 2
    bounds = starts_of(lengths_ref)
    row = lax.broadcasted_iota(I32, (tokens, 128), 0)
    lane = lax.broadcasted_iota(I32, (tokens, 128), 1)
    owner = jnp.full((tokens, 128), -1, I32)
    factor = jnp.zeros((tokens, 128), F32)
    for s in range(SEQS):
        inside = (row >= bounds[s]) & (row < bounds[s + 1])
        total = jnp.full((8, 128), adv_ref[0, s], F32) / jnp.full((8, 128), lengths_ref[0, s], I32).astype(F32)
        owner = jnp.where(inside, policy_ref[0, s], owner)
        factor = jnp.where(inside, total[0:1, :], factor)
    ratio = jnp.clip(jnp.exp(new_ref[...] - old_ref[...]), CLIP_LOW, CLIP_HIGH) * ADAPTER_SCALE
    groups = ratio.shape[0]
    ratio = jnp.concatenate([ratio, jnp.zeros((128 - groups, 128), F32)], axis=0).T
    ratio = jnp.concatenate([ratio[:, j : j + 1] for j in range(groups)], axis=0)
    weight = factor * ratio

    def own(full):
        total = jnp.zeros((tokens, 128), F32)
        for j in range(POLICIES // 2):
            mine = owner == 2 * j + jnp.where(lane >= RANK, 1, 0)
            total = total + jnp.where(mine, full[:, j * 128 : (j + 1) * 128], 0.0)
        return total + pltpu.roll(total, RANK, 1)

    low_in = own(jnp.dot(acts_ref[...], down_ref[...], preferred_element_type=F32))
    low_out = own(
        lax.dot_general(cot_ref[...], up_ref[...], (((1,), (1,)), ((), ())), preferred_element_type=F32)
    )
    x_ref[...] = jnp.where(lane < RANK, low_in, low_out) * weight
    core = lax.rem(lax.axis_index("mp"), 2)
    keep_ref[...] = x_ref[pl.ds(pl.multiple_of(core * half, half), half), :]
    send_ref[...] = x_ref[pl.ds(pl.multiple_of((1 - core) * half, half), half), :]


BLOCKS = 4


def pack_kernel(keep_ref, got_ref, sum_ref, out_ref):
    half = keep_ref.shape[0]
    step = half // BLOCKS
    total = keep_ref[...] + got_ref[...]
    sum_ref[...] = total
    codes = []
    for b in range(BLOCKS):
        part = total[b * step : (b + 1) * step]
        code = code_of(jnp.max(jnp.abs(part), axis=0, keepdims=True))
        codes.append(code)
        out_ref[b * step : (b + 1) * step, :] = to_i16(part * (TOP / scale_of(code)))
    codes.append(jnp.zeros((16 - BLOCKS, 128), F32))
    out_ref[half:, :] = jnp.concatenate(codes, axis=0).astype(I32).astype(I16)


def unpack_kernel(sum_ref, got_ref, out_ref):
    half = sum_ref.shape[0]
    step = half // BLOCKS
    scale = scale_of(from_i16(got_ref[half:, :])) * (1.0 / TOP)
    for b in range(BLOCKS):
        at = slice(b * step, (b + 1) * step)
        out_ref[at, :] = sum_ref[at, :] + from_i16(got_ref[at, :]) * scale[b : b + 1]


def quantize(values_a, values_b, width_a):
    code_a = code_of(jnp.max(jnp.abs(values_a), axis=1, keepdims=True))
    code_b = code_of(jnp.max(jnp.abs(values_b), axis=1, keepdims=True))
    lane = lax.broadcasted_iota(I32, (values_a.shape[0], 128), 1)
    codes = jnp.where(lane < 64, code_a, code_b)
    inverse = TOP / scale_of(codes)
    q_a = to_i16(values_a * inverse[:, 0:1])
    q_b = to_i16(values_b * inverse[:, 64:65])
    return q_a, q_b, codes.astype(I32).astype(I16)


def grad_kernel(lengths_ref, policy_ref, mine_ref, other_ref, acts_ref, cot_ref, out_ref, full_ref, fa_ref, fb_ref):
    tokens, wide_a = acts_ref.shape
    wide_b = cot_ref.shape[1]
    half = tokens // 2
    core = lax.rem(lax.axis_index("mp"), 2)
    full_ref[pl.ds(pl.multiple_of(core * half, half), half), :] = mine_ref[...]
    full_ref[pl.ds(pl.multiple_of((1 - core) * half, half), half), :] = other_ref[...]
    low = full_ref[...].T
    bounds = starts_of(lengths_ref)
    pos = lax.broadcasted_iota(I32, (POLICIES * 4, tokens), 1)
    member = lax.broadcasted_iota(I32, (POLICIES * 4, tokens), 0) // 4
    owner = jnp.full((POLICIES * 4, tokens), -1, I32)
    for s in range(SEQS):
        owner = jnp.where((pos >= bounds[s]) & (pos < bounds[s + 1]), policy_ref[0, s], owner)
    mask = owner == member

    def wide(rows):
        groups = []
        for k in range(4):
            for d in range(4):
                first = rows[k * 16 + d * 4 : k * 16 + d * 4 + 4]
                second = rows[d * 16 + k * 4 : d * 16 + k * 4 + 4]
                part = jnp.where(core == 0, first, second)
                part = jnp.concatenate([part] * POLICIES, axis=0)
                groups.append(jnp.where(mask, part, 0.0))
        both = jnp.concatenate(groups, axis=0)
        high = both.astype(BF16)
        return high, (both - high.astype(F32)).astype(BF16)

    for rows, x_ref, f_ref in ((low[RANK:], acts_ref, fa_ref), (low[:RANK], cot_ref, fb_ref)):
        high, rest = wide(rows)
        width = x_ref.shape[1]
        for c0 in range(0, width, 256):
            c1 = min(c0 + 256, width)
            x = x_ref[:, c0:c1]
            f_ref[:, c0:c1] = jnp.dot(high, x, preferred_element_type=F32) + jnp.dot(
                rest, x, preferred_element_type=F32
            )
    step = out_ref.shape[1]
    for k in range(4):
        at = slice(k * step, (k + 1) * step)
        q_a, q_b, codes = quantize(fa_ref[at, :], fb_ref[at, :], wide_a)
        out_ref[k, :, :wide_a] = q_a
        out_ref[k, :, wide_a : wide_a + wide_b] = q_b
        out_ref[k, :, wide_a + wide_b :] = codes


def sum_parts(got_ref, wide_a, wide_b):
    total_a = total_b = None
    for k in range(got_ref.shape[0]):
        scale = scale_of(from_i16(got_ref[k, :, wide_a + wide_b :])) * (1.0 / TOP)
        a = from_i16(got_ref[k, :, :wide_a]) * scale[:, 0:1]
        b = from_i16(got_ref[k, :, wide_a : wide_a + wide_b]) * scale[:, 64:65]
        total_a = a if total_a is None else total_a + a
        total_b = b if total_b is None else total_b + b
    return total_a, total_b


def second_kernel(wide_a, wide_b, got_ref, out_ref):
    total_a, total_b = sum_parts(got_ref, wide_a, wide_b)
    q_a, q_b, codes = quantize(total_a, total_b, wide_a)
    rows = out_ref.shape[1]
    for k in range(4):
        at = slice(k * rows, (k + 1) * rows)
        out_ref[k, :, :wide_a] = q_a[at]
        out_ref[k, :, wide_a : wide_a + wide_b] = q_b[at]
        out_ref[k, :, wide_a + wide_b :] = codes[at]


def third_kernel(wide_a, wide_b, got_ref, out_ref):
    total_a, total_b = sum_parts(got_ref, wide_a, wide_b)
    for p in range(POLICIES):
        a = total_a[p * 4 : (p + 1) * 4]
        b = total_b[p * 4 : (p + 1) * 4]
        code_a = code_of(jnp.max(jnp.abs(a)).reshape(1, 1))
        code_b = code_of(jnp.max(jnp.abs(b)).reshape(1, 1))
        pieces = [a[:, c : c + 128] * (TOP / scale_of(code_a)) for c in range(0, wide_a, 128)]
        pieces += [b[:, c : c + 128] * (TOP / scale_of(code_b)) for c in range(0, wide_b, 128)]
        pieces.append(jnp.broadcast_to(code_a, (4, 128)))
        pieces.append(jnp.broadcast_to(code_b, (4, 128)))
        pieces.append(jnp.zeros((4, 128), F32))
        out_ref[p] = to_i16(jnp.concatenate(pieces, axis=0))


def last_kernel(wide_a, wide_b, got_ref, a_ref, b_ref):
    n_a, n_b = wide_a // 128, wide_b // 128
    total = None
    for k in range(POLICIES):
        values = from_i16(got_ref[k])
        at = 4 * (n_a + n_b)
        s_a = scale_of(values[at : at + 1]) * (1.0 / TOP)
        s_b = scale_of(values[at + 4 : at + 5]) * (1.0 / TOP)
        row = lax.broadcasted_iota(I32, values.shape, 0)
        values = values * jnp.where(row < 4 * n_a, s_a, s_b)
        total = values if total is None else total + values
    for c in range(n_a):
        a_ref[:, c * 128 : (c + 1) * 128] = total[c * 4 : (c + 1) * 4]
    for c in range(n_b):
        b_ref[:, c * 128 : (c + 1) * 128] = total[4 * (n_a + c) : 4 * (n_a + c + 1)]


def call(kernel, outs, n_smem, n_vmem, scratch=(), flops=0):
    return pl.pallas_call(
        kernel,
        out_shape=[jax.ShapeDtypeStruct(s, d) for s, d in outs],
        in_specs=[SMEM] * n_smem + [VMEM] * n_vmem,
        out_specs=[VMEM] * len(outs),
        scratch_shapes=[pltpu.VMEM(s, d) for s, d in scratch],
        compiler_params=pltpu.CompilerParams(vmem_limit_bytes=40 * 1024 * 1024),
    )


def groups_of():
    index = np.arange(512).reshape(8, 4, 4, 2, 2)
    first, second = [], []
    for z in range(8):
        for h in range(2):
            for k in range(4):
                first.append(index[z, :, k, h, 0].tolist())
                first.append(index[z, k, :, h, 1].tolist())
                second.append(index[z, k, :, h, 0].tolist())
                second.append(index[z, :, k, h, 1].tolist())
    third = [index[:, x, y, h, c].tolist() for x in range(4) for y in range(4) for h in range(2) for c in range(2)]
    return first, second, third


def shards(acts, cot, lengths, policy, advantages, old, new, down, up):
    tokens, wide_a = acts.shape
    wide_b = cot.shape[1]
    half = tokens // 2
    first, second, third = groups_of()
    core_pairs = [(0, 1), (1, 0), (2, 3), (3, 2)]
    far_pairs = [(0, 2), (2, 0), (1, 3), (3, 1)]
    keep, send = call(
        low_kernel, [((half, 128), F32)] * 2, 3, 6, [((tokens, 128), F32)]
    )(lengths, policy, advantages, old.reshape(tokens // 128, 128), new.reshape(tokens // 128, 128), acts, cot, down, up)
    got = lax.ppermute(send, "mp", core_pairs)
    part, packed = call(pack_kernel, [((half, 128), F32), ((half + 16, 128), I16)], 0, 2)(keep, got)
    far = lax.ppermute(packed, "mp", far_pairs)
    (mine,) = call(unpack_kernel, [((half, 128), F32)], 0, 2)(part, far)
    other = lax.ppermute(mine, "mp", core_pairs)
    rows = POLICIES * RANK
    width = wide_a + wide_b + 128
    (pieces,) = call(
        grad_kernel,
        [((4, rows // 4, width), I16)],
        2,
        4,
        [((tokens, 128), F32), ((rows, wide_a), F32), ((rows, wide_b), F32)],
    )(lengths, policy, mine, other, acts, cot)
    got = lax.all_to_all(pieces, BOTH, 0, 0, tiled=True, axis_index_groups=first)
    (pieces,) = call(
        functools.partial(second_kernel, wide_a, wide_b), [((4, rows // 16, width), I16)], 0, 1
    )(got)
    got = lax.all_to_all(pieces, BOTH, 0, 0, tiled=True, axis_index_groups=second)
    deep = 4 * (wide_a + wide_b) // 128 + 12
    (pieces,) = call(
        functools.partial(third_kernel, wide_a, wide_b), [((POLICIES, deep, 128), I16)], 0, 1
    )(got)
    got = lax.all_to_all(pieces, BOTH, 0, 0, tiled=True, axis_index_groups=third)
    return tuple(
        call(
            functools.partial(last_kernel, wide_a, wide_b), [((4, wide_a), F32), ((4, wide_b), F32)], 0, 1
        )(got)
    )


def solution(mesh):
    return jax.shard_map(
        shards,
        mesh=mesh,
        in_specs=(
            P("dp", "mp"),
            P("dp", "mp"),
            P("dp", None),
            P("dp", None),
            P("dp", None),
            P("dp"),
            P("dp"),
            P("mp", None),
            P(None, "mp"),
        ),
        out_specs=(P("dp", "mp"), P("dp", "mp")),
        check_vma=False,
    )
```

time: 2170 us -> 94.5 us (0.04)
  the two profiles are of different devices: /device:TPU:0 before, /device:TPU:2 now
where the time goes in v1:
time: 94.5 us; the launch traced here: 94 us
  blocking collectives  52.6 us (56%)
  starting transfers between devices  19.6 us (21%)
  local copies, waits for them, and re-layouts  7.96 us (8%)
  Pallas kernels  7.72 us (8%)
  waiting for transfers between devices  5.41 us (6%)
    all_to_all x1, blocking collectives, shards(): lax.all_to_all(pieces, BOTH, 0, 0, tiled=True, axis_index_groups=third)  22.3 us
    all_to_all x1, blocking collectives, shards(): lax.all_to_all(pieces, BOTH, 0, 0, tiled=True, axis_index_groups=first)  18.4 us
    ppermute x1, starting transfers between devices, shards(): far = lax.ppermute(packed, 'mp', far_pairs)  15.7 us
    all_to_all x1, blocking collectives, shards(): lax.all_to_all(pieces, BOTH, 0, 0, tiled=True, axis_index_groups=second)  11.8 us
    unnamed x26, local copies, waits for them, and re-layouts  7.96 us
    pallas_call x1, Pallas kernels, shards(): call(grad_kernel, [((4, rows // 4, width), I16)], 2, 4, [((tokens, 128),...  3.42 us
    ppermute x1, waiting for transfers between devices, shards(): far = lax.ppermute(packed, 'mp', far_pairs)  2.78 us
    pallas_call x1, Pallas kernels, shards(): call(low_kernel, [((half, 128), F32)] * 2, 3, 6, [((tokens, 128), F32)])  2.47 us
  transfers between devices with their start and end apart: 3, of which 3 were waited for; matrix products, arithmetic and copies ran while one was open for 0% of the time, Pallas kernels for 0%

profile of v1, /device:TPU:2, one launch (start us, length us, event | category | flops | bytes accessed | tf_op | source)
XLA Modules:
  0.0 94.0 jit_solution(9098379732808477833)
XLA Ops:
  0.6 0.0 copy-start
  0.6 1.3 %copy-done = bf16[512,1152]{1,0:T(8,128)(2,1)S(1)} copy-done((bf16[512,1152]{1,0:T(8,128)(2,1)S(1)}, bf16[512,1152]{1,0:T(8,128)(2,1)}, u32[]{:S(2)}) %copy-start) | copy-done | bytes 1179672
  1.9 0.0 copy-start.2
  1.9 1.0 %copy-done.2 = bf16[512,512]{1,0:T(8,128)(2,1)S(1)} copy-done((bf16[512,512]{1,0:T(8,128)(2,1)S(1)}, bf16[512,512]{1,0:T(8,128)(2,1)}, u32[]{:S(2)}) %copy-start.2) | copy-done | bytes 524312
  2.9 0.0 copy-start.4
  2.9 1.3 %copy-done.4 = bf16[1152,512]{1,0:T(8,128)(2,1)S(1)} copy-done((bf16[1152,512]{1,0:T(8,128)(2,1)S(1)}, bf16[1152,512]{1,0:T(8,128)(2,1)}, u32[]{:S(2)}) %copy-start.4) | copy-done | bytes 1179672
  4.2 0.0 copy-start.5
  4.2 1.0 %copy-done.5 = bf16[512,512]{1,0:T(8,128)(2,1)S(1)} copy-done((bf16[512,512]{1,0:T(8,128)(2,1)S(1)}, bf16[512,512]{1,0:T(8,128)(2,1)}, u32[]{:S(2)}) %copy-start.5) | copy-done | bytes 524312
  5.3 0.0 copy-start.6
  5.3 0.7 copy-done.6
  5.9 0.0 copy-start.7
  5.9 0.7 copy-done.7
  6.6 0.0 copy-start.8
  6.6 0.7 copy-done.8
  7.3 0.0 copy-start.10
  7.3 0.7 copy-done.10
  7.9 0.0 copy-start.12
  7.9 0.7 copy-done.12
  8.6 0.0 copy-start.1
  8.6 0.0 copy-start.3
  8.6 0.0 copy-start.9
  8.6 0.0 copy-start.11
  8.6 2.5 %shard_map.104 = (f32[256,128]{1,0:T(8,128)S(1)}, f32[256,128]{1,0:T(8,128)S(1)}) custom-call(s32[1,8]{1,0:T(1,128)S(1)} %copy-done.8, s32[1,8]{1,0:T(1,128)S(1)} %copy-done.10, f32[1,8]{1,0:T(1,128)S(1)} %copy-done.12, f32[4,128]{1,0:T(4,128)S(1)} %bitcast.2, f32[4,128]{1,0:T(4,128)S(1)} %bitcast.3, bf16[512,1152]{1,0:T(8,128)(2,1)S(1)} %copy-done, ...), custom_call_target="tpu_custom_call" | custom-call | tf_op jit(solution)/shard_map/pallas_call | solution.py:257
  11.1 1.9 %collective-permute-start = (f32[256,128]{1,0:T(8,128)S(1)}, f32[256,128]{1,0:T(8,128)S(1)}, u32[]{:S(2)}, u32[]{:S(2)}) collective-permute-start(f32[256,128]{1,0:T(8,128)S(1)} %get-tuple-element.7), channel_id=1, source_target_pairs={{0,1},{1,0},{2,3},{3,2},{4,5},{5,4},{6,7},{7,6},{8,9},{9,8},{10,11... | collective-permute-start | bytes 393224 | tf_op jit(solution)/shard_map/ppermute | solution.py:260
  13.0 1.3 %collective-permute-done.got_ref = f32[256,128]{1,0:T(8,128)S(1)} collective-permute-done((f32[256,128]{1,0:T(8,128)S(1)}, f32[256,128]{1,0:T(8,128)S(1)}, u32[]{:S(2)}, u32[]{:S(2)}) %collective-permute-start) | collective-permute-done | bytes 131104 | tf_op jit(solution)/shard_map/ppermute | solution.py:260
  14.3 0.1 shard_map.105
  14.4 15.7 %collective-permute-start.1 = (s16[272,128]{1,0:T(8,128)(2,1)S(1)}, s16[272,128]{1,0:T(8,128)(2,1)S(1)}, u32[]{:S(2)}, u32[]{:S(2)}) collective-permute-start(s16[272,128]{1,0:T(8,128)(2,1)S(1)} %get-tuple-element.9), channel_id=1, source_target_pairs={{0,2},{2,0},{1,3},{3,1},{4,6},{6,4},{5,7},{7,5},{8,10},{10,8},{9,1... | collective-permute-start | bytes 208904 | tf_op jit(solution)/shard_map/ppermute | solution.py:262
  30.1 2.8 %collective-permute-done.1.got_ref = s16[272,128]{1,0:T(8,128)(2,1)S(1)} collective-permute-done((s16[272,128]{1,0:T(8,128)(2,1)S(1)}, s16[272,128]{1,0:T(8,128)(2,1)S(1)}, u32[]{:S(2)}, u32[]{:S(2)}) %collective-permute-start.1) | collective-permute-done | bytes 69664 | tf_op jit(solution)/shard_map/ppermute | solution.py:262
  32.9 1.9 %collective-permute-start.2 = (f32[256,128]{1,0:T(8,128)S(1)}, f32[256,128]{1,0:T(8,128)S(1)}, u32[]{:S(2)}, u32[]{:S(2)}) collective-permute-start(f32[256,128]{1,0:T(8,128)S(1)} %shard_map.106.mine_ref), channel_id=1, source_target_pairs={{0,1},{1,0},{2,3},{3,2},{4,5},{5,4},{6,7},{7,6},{8,9},{9,8},{10,11... | collective-permute-start | bytes 393224 | tf_op jit(solution)/shard_map/ppermute | solution.py:264
  34.9 1.3 %collective-permute-done.2.other_ref = f32[256,128]{1,0:T(8,128)S(1)} collective-permute-done((f32[256,128]{1,0:T(8,128)S(1)}, f32[256,128]{1,0:T(8,128)S(1)}, u32[]{:S(2)}, u32[]{:S(2)}) %collective-permute-start.2) | collective-permute-done | bytes 131104 | tf_op jit(solution)/shard_map/ppermute | solution.py:264
  36.2 0.0 copy-done.1
  36.2 0.0 copy-done.3
  36.2 0.0 copy-done.9
  36.2 0.0 copy-done.11
  36.2 3.4 %shard_map.107 = s16[4,128,1792]{2,1,0:T(8,128)(2,1)S(1)} custom-call(s32[1,8]{1,0:T(1,128)S(1)} %copy-done.9, s32[1,8]{1,0:T(1,128)S(1)} %copy-done.11, f32[256,128]{1,0:T(8,128)S(1)} %shard_map.106.mine_ref, f32[256,128]{1,0:T(8,128)S(1)} %collective-permute-done.2.other_ref, bf16[512,1152]{1,0:T(8,128)(2,1)S(1)} %copy-done.1, bf16[512,512]{1,0:T(8,128)(2,1)S(1)} %copy-done.3), custom_call_target="tpu_custom_call" | custom-call | tf_op jit(solution)/shard_map/pallas_call | solution.py:267
  39.6 18.4 %all_to_all.15.got_ref = s16[4,128,1792]{2,1,0:T(8,128)(2,1)S(1)} all-to-all(s16[4,128,1792]{2,1,0:T(8,128)(2,1)S(1)} %shard_map.107), channel_id=1, replica_groups={{0,16,32,48},{1,5,9,13},{4,20,36,52},{17,21,25,29},{8,24,40,56},{33,37,..., dimensions={0} | all-to-all | bytes 3670016 | tf_op jit(solution)/shard_map/all_to_all | solution.py:274
  58.1 0.7 shard_map.108
  58.8 11.8 %all_to_all.16.got_ref = s16[4,32,1792]{2,1,0:T(8,128)(2,1)S(1)} all-to-all(s16[4,32,1792]{2,1,0:T(8,128)(2,1)S(1)} %shard_map.108), channel_id=1, replica_groups={{0,4,8,12},{1,17,33,49},{16,20,24,28},{5,21,37,53},{32,36,40,44},{9,25,..., dimensions={0} | all-to-all | bytes 917504 | tf_op jit(solution)/shard_map/all_to_all | solution.py:278
  70.6 0.4 shard_map.109
  71.0 22.3 %all_to_all.17.got_ref = s16[8,64,128]{2,1,0:T(8,128)(2,1)S(1)} all-to-all(s16[8,64,128]{2,1,0:T(8,128)(2,1)S(1)} %shard_map.109), channel_id=1, replica_groups={{0,64,128,192,256,320,384,448},{1,65,129,193,257,321,385,449},{2,66,130..., dimensions={0} | all-to-all | bytes 262144 | tf_op jit(solution)/shard_map/all_to_all | solution.py:283
  93.3 0.7 shard_map.110
  (1 shorter events, 0.0 us)
Async XLA Ops:
  0.6 1.3 %copy-start = (bf16[512,1152]{1,0:T(8,128)(2,1)S(1)}, bf16[512,1152]{1,0:T(8,128)(2,1)}, u32[]{:S(2)}) copy-start(bf16[512,1152]{1,0:T(8,128)(2,1)} %acts_ref.3) | copy-start | bytes 3538948
  1.9 1.0 %copy-start.2 = (bf16[512,512]{1,0:T(8,128)(2,1)S(1)}, bf16[512,512]{1,0:T(8,128)(2,1)}, u32[]{:S(2)}) copy-start(bf16[512,512]{1,0:T(8,128)(2,1)} %cot_ref.3) | copy-start | bytes 1572868
  2.9 1.3 %copy-start.4 = (bf16[1152,512]{1,0:T(8,128)(2,1)S(1)}, bf16[1152,512]{1,0:T(8,128)(2,1)}, u32[]{:S(2)}) copy-start(bf16[1152,512]{1,0:T(8,128)(2,1)} %down_ref.1) | copy-start | bytes 3538948
  4.2 1.0 %copy-start.5 = (bf16[512,512]{1,0:T(8,128)(2,1)S(1)}, bf16[512,512]{1,0:T(8,128)(2,1)}, u32[]{:S(2)}) copy-start(bf16[512,512]{1,0:T(8,128)(2,1)} %up_ref.1) | copy-start | bytes 1572868
  5.3 0.7 copy-start.6
  5.9 0.7 copy-start.7
  6.6 0.7 copy-start.8
  7.3 0.7 copy-start.10
  7.9 0.7 copy-start.12
  8.6 27.6 %copy-start.1 = (bf16[512,1152]{1,0:T(8,128)(2,1)S(1)}, bf16[512,1152]{1,0:T(8,128)(2,1)}, u32[]{:S(2)}) copy-start(bf16[512,1152]{1,0:T(8,128)(2,1)} %acts_ref.3) | copy-start | bytes 3538948
  8.6 27.6 %copy-start.3 = (bf16[512,512]{1,0:T(8,128)(2,1)S(1)}, bf16[512,512]{1,0:T(8,128)(2,1)}, u32[]{:S(2)}) copy-start(bf16[512,512]{1,0:T(8,128)(2,1)} %cot_ref.3) | copy-start | bytes 1572868
  8.6 27.6 %copy-start.9 = (s32[1,8]{1,0:T(1,128)S(1)}, s32[1,8]{1,0:T(1,128)}, u32[]{:S(2)}) copy-start(s32[1,8]{1,0:T(1,128)} %lengths_ref.3) | copy-start | bytes 100
  8.6 27.6 %copy-start.11 = (s32[1,8]{1,0:T(1,128)S(1)}, s32[1,8]{1,0:T(1,128)}, u32[]{:S(2)}) copy-start(s32[1,8]{1,0:T(1,128)} %policy_ref.3) | copy-start | bytes 100
  11.1 3.2 %collective-permute-start = (f32[256,128]{1,0:T(8,128)S(1)}, f32[256,128]{1,0:T(8,128)S(1)}, u32[]{:S(2)}, u32[]{:S(2)}) collective-permute-start(f32[256,128]{1,0:T(8,128)S(1)} %get-tuple-element.7), channel_id=1, source_target_pairs={{0,1},{1,0},{2,3},{3,2},{4,5},{5,4},{6,7},{7,6},{8,9},{9,8},{10,11... | collective-permute-start | bytes 393224 | tf_op jit(solution)/shard_map/ppermute | solution.py:260
  14.4 18.5 %collective-permute-start.1 = (s16[272,128]{1,0:T(8,128)(2,1)S(1)}, s16[272,128]{1,0:T(8,128)(2,1)S(1)}, u32[]{:S(2)}, u32[]{:S(2)}) collective-permute-start(s16[272,128]{1,0:T(8,128)(2,1)S(1)} %get-tuple-element.9), channel_id=1, source_target_pairs={{0,2},{2,0},{1,3},{3,1},{4,6},{6,4},{5,7},{7,5},{8,10},{10,8},{9,1... | collective-permute-start | bytes 208904 | tf_op jit(solution)/shard_map/ppermute | solution.py:262
  32.9 3.2 %collective-permute-start.2 = (f32[256,128]{1,0:T(8,128)S(1)}, f32[256,128]{1,0:T(8,128)S(1)}, u32[]{:S(2)}, u32[]{:S(2)}) collective-permute-start(f32[256,128]{1,0:T(8,128)S(1)} %shard_map.106.mine_ref), channel_id=1, source_target_pairs={{0,1},{1,0},{2,3},{3,2},{4,5},{5,4},{6,7},{7,6},{8,9},{9,8},{10,11... | collective-permute-start | bytes 393224 | tf_op jit(solution)/shard_map/ppermute | solution.py:264

commit v2 on v1

--- a/solution.py
+++ b/solution.py
@@ -18,8 +18,7 @@
 TOP = 32767.0
 F32, BF16, I16, I32 = jnp.float32, jnp.bfloat16, jnp.int16, jnp.int32
 BOTH = ("dp", "mp")
-VMEM = pl.BlockSpec(memory_space=pltpu.VMEM)
-SMEM = pl.BlockSpec(memory_space=pltpu.SMEM)
+VMEM, SMEM, HBM = pltpu.VMEM, pltpu.SMEM, pltpu.HBM
 
 
 def code_of(largest):
@@ -31,7 +30,7 @@
 
 
 def to_i16(values):
-    return jnp.clip(jnp.round(values), -TOP, TOP).astype(I32).astype(I16)
+    return jnp.round(values).astype(I32).astype(I16)
 
 
 def from_i16(values):
@@ -45,11 +44,34 @@
     return bounds
 
 
+CUT = 512
+
+
 def low_kernel(
-    lengths_ref, policy_ref, adv_ref, old_ref, new_ref, acts_ref, cot_ref, down_ref, up_ref, keep_ref, send_ref, x_ref
+    lengths_hbm, policy_hbm, adv_hbm, old_hbm, new_hbm, acts_hbm, cot_hbm, down_hbm, up_hbm,
+    keep_ref, send_ref,
+    x_ref, lengths_ref, policy_ref, adv_ref, old_ref, new_ref, acts_ref, cot_ref, down_ref, up_ref, sems,
 ):
-    tokens = acts_ref.shape[0]
+    tokens, wide_a = acts_ref.shape
     half = tokens // 2
+    pairs = [
+        (lengths_hbm, lengths_ref),
+        (policy_hbm, policy_ref),
+        (adv_hbm, adv_ref),
+        (old_hbm, old_ref),
+        (new_hbm, new_ref),
+        (cot_hbm, cot_ref),
+        (up_hbm, up_ref),
+        (acts_hbm.at[:, :CUT], acts_ref.at[:, :CUT]),
+        (down_hbm.at[:CUT, :], down_ref.at[:CUT, :]),
+        (acts_hbm.at[:, CUT:], acts_ref.at[:, CUT:]),
+        (down_hbm.at[CUT:, :], down_ref.at[CUT:, :]),
+    ]
+    copies = [pltpu.make_async_copy(src, dst, sems.at[i]) for i, (src, dst) in enumerate(pairs)]
+    for copy in copies:
+        copy.start()
+    for copy in copies[:5]:
+        copy.wait()
     bounds = starts_of(lengths_ref)
     row = lax.broadcasted_iota(I32, (tokens, 128), 0)
     lane = lax.broadcasted_iota(I32, (tokens, 128), 1)
@@ -73,10 +95,17 @@
             total = total + jnp.where(mine, full[:, j * 128 : (j + 1) * 128], 0.0)
         return total + pltpu.roll(total, RANK, 1)
 
-    low_in = own(jnp.dot(acts_ref[...], down_ref[...], preferred_element_type=F32))
+    copies[5].wait()
+    copies[6].wait()
     low_out = own(
         lax.dot_general(cot_ref[...], up_ref[...], (((1,), (1,)), ((), ())), preferred_element_type=F32)
     )
+    copies[7].wait()
+    copies[8].wait()
+    low_in = jnp.dot(acts_ref[:, :CUT], down_ref[:CUT, :], preferred_element_type=F32)
+    copies[9].wait()
+    copies[10].wait()
+    low_in = own(low_in + jnp.dot(acts_ref[:, CUT:], down_ref[CUT:, :], preferred_element_type=F32))
     x_ref[...] = jnp.where(lane < RANK, low_in, low_out) * weight
     core = lax.rem(lax.axis_index("mp"), 2)
     keep_ref[...] = x_ref[pl.ds(pl.multiple_of(core * half, half), half), :]
@@ -222,15 +251,19 @@
         b_ref[:, c * 128 : (c + 1) * 128] = total[4 * (n_a + c) : 4 * (n_a + c + 1)]
 
 
-def call(kernel, outs, n_smem, n_vmem, scratch=(), flops=0):
+def call(kernel, outs, spaces, scratch=()):
     return pl.pallas_call(
         kernel,
         out_shape=[jax.ShapeDtypeStruct(s, d) for s, d in outs],
-        in_specs=[SMEM] * n_smem + [VMEM] * n_vmem,
-        out_specs=[VMEM] * len(outs),
-        scratch_shapes=[pltpu.VMEM(s, d) for s, d in scratch],
+        in_specs=[pl.BlockSpec(memory_space=m) for m in spaces],
+        out_specs=[pl.BlockSpec(memory_space=pltpu.VMEM)] * len(outs),
+        scratch_shapes=list(scratch),
         compiler_params=pltpu.CompilerParams(vmem_limit_bytes=40 * 1024 * 1024),
     )
+
+
+def in_hbm(array):
+    return pltpu.with_memory_space_constraint(array, pltpu.HBM)
 
 
 def groups_of():
@@ -254,36 +287,51 @@
     first, second, third = groups_of()
     core_pairs = [(0, 1), (1, 0), (2, 3), (3, 2)]
     far_pairs = [(0, 2), (2, 0), (1, 3), (3, 1)]
+    lines = (tokens // 128, 128)
     keep, send = call(
-        low_kernel, [((half, 128), F32)] * 2, 3, 6, [((tokens, 128), F32)]
-    )(lengths, policy, advantages, old.reshape(tokens // 128, 128), new.reshape(tokens // 128, 128), acts, cot, down, up)
+        low_kernel,
+        [((half, 128), F32)] * 2,
+        [HBM] * 9,
+        [
+            VMEM((tokens, 128), F32),
+            SMEM(lengths.shape, I32),
+            SMEM(policy.shape, I32),
+            SMEM(advantages.shape, F32),
+            VMEM(lines, F32),
+            VMEM(lines, F32),
+            VMEM(acts.shape, BF16),
+            VMEM(cot.shape, BF16),
+            VMEM(down.shape, BF16),
+            VMEM(up.shape, BF16),
+            pltpu.SemaphoreType.DMA((11,)),
+        ],
+    )(*map(in_hbm, (lengths, policy, advantages, old.reshape(lines), new.reshape(lines), acts, cot, down, up)))
     got = lax.ppermute(send, "mp", core_pairs)
-    part, packed = call(pack_kernel, [((half, 128), F32), ((half + 16, 128), I16)], 0, 2)(keep, got)
+    part, packed = call(pack_kernel, [((half, 128), F32), ((half + 16, 128), I16)], [VMEM] * 2)(keep, got)
     far = lax.ppermute(packed, "mp", far_pairs)
-    (mine,) = call(unpack_kernel, [((half, 128), F32)], 0, 2)(part, far)
+    (mine,) = call(unpack_kernel, [((half, 128), F32)], [VMEM] * 2)(part, far)
     other = lax.ppermute(mine, "mp", core_pairs)
     rows = POLICIES * RANK
     width = wide_a + wide_b + 128
     (pieces,) = call(
         grad_kernel,
         [((4, rows // 4, width), I16)],
-        2,
-        4,
-        [((tokens, 128), F32), ((rows, wide_a), F32), ((rows, wide_b), F32)],
+        [SMEM] * 2 + [VMEM] * 4,
+        [VMEM((tokens, 128), F32), VMEM((rows, wide_a), F32), VMEM((rows, wide_b), F32)],
     )(lengths, policy, mine, other, acts, cot)
     got = lax.all_to_all(pieces, BOTH, 0, 0, tiled=True, axis_index_groups=first)
     (pieces,) = call(
-        functools.partial(second_kernel, wide_a, wide_b), [((4, rows // 16, width), I16)], 0, 1
+        functools.partial(second_kernel, wide_a, wide_b), [((4, rows // 16, width), I16)], [VMEM]
     )(got)
     got = lax.all_to_all(pieces, BOTH, 0, 0, tiled=True, axis_index_groups=second)
     deep = 4 * (wide_a + wide_b) // 128 + 12
     (pieces,) = call(
-        functools.partial(third_kernel, wide_a, wide_b), [((POLICIES, deep, 128), I16)], 0, 1
+        functools.partial(third_kernel, wide_a, wide_b), [((POLICIES, deep, 128), I16)], [VMEM]
     )(got)
     got = lax.all_to_all(pieces, BOTH, 0, 0, tiled=True, axis_index_groups=third)
     return tuple(
         call(
-            functools.partial(last_kernel, wide_a, wide_b), [((4, wide_a), F32), ((4, wide_b), F32)], 0, 1
+            functools.partial(last_kernel, wide_a, wide_b), [((4, wide_a), F32), ((4, wide_b), F32)], [VMEM]
         )(got)
     )
 

time: 94.5 us -> 87 us (0.921)
  local copies, waits for them, and re-layouts: 7.96 us -> 0.02 us
    unnamed x26 -> x8, local copies, waits for them, and re-layouts: 7.96 us -> 0.02 us
where the time goes in v2:
time: 87 us; the launch traced here: 86.7 us
  blocking collectives  52.7 us (61%)
  starting transfers between devices  19.6 us (23%)
  Pallas kernels  8.27 us (10%)
  waiting for transfers between devices  5.41 us (6%)
    all_to_all x1, blocking collectives, shards(): lax.all_to_all(pieces, BOTH, 0, 0, tiled=True, axis_index_groups=third)  22.5 us
    all_to_all x1, blocking collectives, shards(): lax.all_to_all(pieces, BOTH, 0, 0, tiled=True, axis_index_groups=first)  18.4 us
    ppermute x1, starting transfers between devices, shards(): far = lax.ppermute(packed, 'mp', far_pairs)  15.7 us
    all_to_all x1, blocking collectives, shards(): lax.all_to_all(pieces, BOTH, 0, 0, tiled=True, axis_index_groups=second)  11.8 us
    pallas_call x1, Pallas kernels, shards(): call(grad_kernel, [((4, rows // 4, width), I16)], [SMEM] * 2 + [VMEM] * 4...  3.34 us
    pallas_call x1, Pallas kernels, shards(): call(low_kernel, [((half, 128), F32)] * 2, [HBM] * 9, [VMEM((tokens, 128)...  3.13 us
    ppermute x1, waiting for transfers between devices, shards(): far = lax.ppermute(packed, 'mp', far_pairs)  2.78 us
    ppermute x1, starting transfers between devices, shards(): other = lax.ppermute(mine, 'mp', core_pairs)  1.92 us
  transfers between devices with their start and end apart: 3, of which 3 were waited for; matrix products, arithmetic and copies ran while one was open for 0% of the time, Pallas kernels for 0%

profile of v2, /device:TPU:2, one launch (start us, length us, event | category | flops | bytes accessed | tf_op | source)
XLA Modules:
  0.0 86.7 jit_solution(14027395655401252333)
XLA Ops:
  0.6 0.0 copy-start
  0.6 0.0 copy-start.1
  0.7 0.0 copy-start.2
  0.7 0.0 copy-start.3
  0.7 3.1 %shard_map.104 = (f32[256,128]{1,0:T(8,128)S(1)}, f32[256,128]{1,0:T(8,128)S(1)}) custom-call(s32[1,8]{1,0:T(1,128)} %lengths_ref.1, s32[1,8]{1,0:T(1,128)} %policy_ref.1, f32[1,8]{1,0:T(1,128)} %adv_hbm.1, f32[4,128]{1,0:T(4,128)} %bitcast.2, f32[4,128]{1,0:T(4,128)} %bitcast.3, bf16[512,1152]{1,0:T(8,128)(2,1)} %acts_ref.1, bf16[512,512]{1,0:T(8,128)(2,1)} %cot_ref.1, ...), custom_call_target="tpu_custom_call" | custom-call | tf_op jit(solution)/shard_map/pallas_call | solution.py:291
  3.8 1.9 %collective-permute-start = (f32[256,128]{1,0:T(8,128)S(1)}, f32[256,128]{1,0:T(8,128)S(1)}, u32[]{:S(2)}, u32[]{:S(2)}) collective-permute-start(f32[256,128]{1,0:T(8,128)S(1)} %get-tuple-element.7), channel_id=1, source_target_pairs={{0,1},{1,0},{2,3},{3,2},{4,5},{5,4},{6,7},{7,6},{8,9},{9,8},{10,11... | collective-permute-start | bytes 393224 | tf_op jit(solution)/shard_map/ppermute | solution.py:309
  5.7 1.3 %collective-permute-done.got_ref = f32[256,128]{1,0:T(8,128)S(1)} collective-permute-done((f32[256,128]{1,0:T(8,128)S(1)}, f32[256,128]{1,0:T(8,128)S(1)}, u32[]{:S(2)}, u32[]{:S(2)}) %collective-permute-start) | collective-permute-done | bytes 131104 | tf_op jit(solution)/shard_map/ppermute | solution.py:309
  7.1 0.1 shard_map.105
  7.1 15.7 %collective-permute-start.1 = (s16[272,128]{1,0:T(8,128)(2,1)S(1)}, s16[272,128]{1,0:T(8,128)(2,1)S(1)}, u32[]{:S(2)}, u32[]{:S(2)}) collective-permute-start(s16[272,128]{1,0:T(8,128)(2,1)S(1)} %get-tuple-element.9), channel_id=1, source_target_pairs={{0,2},{2,0},{1,3},{3,1},{4,6},{6,4},{5,7},{7,5},{8,10},{10,8},{9,1... | collective-permute-start | bytes 208904 | tf_op jit(solution)/shard_map/ppermute | solution.py:311
  22.9 2.8 %collective-permute-done.1.got_ref = s16[272,128]{1,0:T(8,128)(2,1)S(1)} collective-permute-done((s16[272,128]{1,0:T(8,128)(2,1)S(1)}, s16[272,128]{1,0:T(8,128)(2,1)S(1)}, u32[]{:S(2)}, u32[]{:S(2)}) %collective-permute-start.1) | collective-permute-done | bytes 69664 | tf_op jit(solution)/shard_map/ppermute | solution.py:311
  25.7 1.9 %collective-permute-start.2 = (f32[256,128]{1,0:T(8,128)S(1)}, f32[256,128]{1,0:T(8,128)S(1)}, u32[]{:S(2)}, u32[]{:S(2)}) collective-permute-start(f32[256,128]{1,0:T(8,128)S(1)} %shard_map.106.mine_ref), channel_id=1, source_target_pairs={{0,1},{1,0},{2,3},{3,2},{4,5},{5,4},{6,7},{7,6},{8,9},{9,8},{10,11... | collective-permute-start | bytes 393224 | tf_op jit(solution)/shard_map/ppermute | solution.py:313
  27.6 1.3 %collective-permute-done.2.other_ref = f32[256,128]{1,0:T(8,128)S(1)} collective-permute-done((f32[256,128]{1,0:T(8,128)S(1)}, f32[256,128]{1,0:T(8,128)S(1)}, u32[]{:S(2)}, u32[]{:S(2)}) %collective-permute-start.2) | collective-permute-done | bytes 131104 | tf_op jit(solution)/shard_map/ppermute | solution.py:313
  28.9 0.0 copy-done
  28.9 0.0 copy-done.1
  28.9 0.0 copy-done.2
  28.9 0.0 copy-done.3
  28.9 3.3 %shard_map.107 = s16[4,128,1792]{2,1,0:T(8,128)(2,1)S(1)} custom-call(s32[1,8]{1,0:T(1,128)S(1)} %copy-done.2, s32[1,8]{1,0:T(1,128)S(1)} %copy-done.3, f32[256,128]{1,0:T(8,128)S(1)} %shard_map.106.mine_ref, f32[256,128]{1,0:T(8,128)S(1)} %collective-permute-done.2.other_ref, bf16[512,1152]{1,0:T(8,128)(2,1)S(1)} %copy-done, bf16[512,512]{1,0:T(8,128)(2,1)S(1)} %copy-done.1), custom_call_target="tpu_custom_call" | custom-call | tf_op jit(solution)/shard_map/pallas_call | solution.py:316
  32.3 18.4 %all_to_all.15.got_ref = s16[4,128,1792]{2,1,0:T(8,128)(2,1)S(1)} all-to-all(s16[4,128,1792]{2,1,0:T(8,128)(2,1)S(1)} %shard_map.107), channel_id=1, replica_groups={{0,16,32,48},{1,5,9,13},{4,20,36,52},{17,21,25,29},{8,24,40,56},{33,37,..., dimensions={0} | all-to-all | bytes 3670016 | tf_op jit(solution)/shard_map/all_to_all | solution.py:322
  50.7 0.7 shard_map.108
  51.4 11.8 %all_to_all.16.got_ref = s16[4,32,1792]{2,1,0:T(8,128)(2,1)S(1)} all-to-all(s16[4,32,1792]{2,1,0:T(8,128)(2,1)S(1)} %shard_map.108), channel_id=1, replica_groups={{0,4,8,12},{1,17,33,49},{16,20,24,28},{5,21,37,53},{32,36,40,44},{9,25,..., dimensions={0} | all-to-all | bytes 917504 | tf_op jit(solution)/shard_map/all_to_all | solution.py:326
  63.2 0.4 shard_map.109
  63.6 22.5 %all_to_all.17.got_ref = s16[8,64,128]{2,1,0:T(8,128)(2,1)S(1)} all-to-all(s16[8,64,128]{2,1,0:T(8,128)(2,1)S(1)} %shard_map.109), channel_id=1, replica_groups={{0,64,128,192,256,320,384,448},{1,65,129,193,257,321,385,449},{2,66,130..., dimensions={0} | all-to-all | bytes 262144 | tf_op jit(solution)/shard_map/all_to_all | solution.py:331
  86.1 0.7 shard_map.110
  (1 shorter events, 0.0 us)
Async XLA Ops:
  0.6 28.3 %copy-start = (bf16[512,1152]{1,0:T(8,128)(2,1)S(1)}, bf16[512,1152]{1,0:T(8,128)(2,1)}, u32[]{:S(2)}) copy-start(bf16[512,1152]{1,0:T(8,128)(2,1)} %acts_ref.1) | copy-start | bytes 3538948
  0.6 28.3 %copy-start.1 = (bf16[512,512]{1,0:T(8,128)(2,1)S(1)}, bf16[512,512]{1,0:T(8,128)(2,1)}, u32[]{:S(2)}) copy-start(bf16[512,512]{1,0:T(8,128)(2,1)} %cot_ref.1) | copy-start | bytes 1572868
  0.7 28.3 %copy-start.2 = (s32[1,8]{1,0:T(1,128)S(1)}, s32[1,8]{1,0:T(1,128)}, u32[]{:S(2)}) copy-start(s32[1,8]{1,0:T(1,128)} %lengths_ref.1) | copy-start | bytes 100
  0.7 28.3 %copy-start.3 = (s32[1,8]{1,0:T(1,128)S(1)}, s32[1,8]{1,0:T(1,128)}, u32[]{:S(2)}) copy-start(s32[1,8]{1,0:T(1,128)} %policy_ref.1) | copy-start | bytes 100
  3.8 3.2 %collective-permute-start = (f32[256,128]{1,0:T(8,128)S(1)}, f32[256,128]{1,0:T(8,128)S(1)}, u32[]{:S(2)}, u32[]{:S(2)}) collective-permute-start(f32[256,128]{1,0:T(8,128)S(1)} %get-tuple-element.7), channel_id=1, source_target_pairs={{0,1},{1,0},{2,3},{3,2},{4,5},{5,4},{6,7},{7,6},{8,9},{9,8},{10,11... | collective-permute-start | bytes 393224 | tf_op jit(solution)/shard_map/ppermute | solution.py:309
  7.1 18.5 %collective-permute-start.1 = (s16[272,128]{1,0:T(8,128)(2,1)S(1)}, s16[272,128]{1,0:T(8,128)(2,1)S(1)}, u32[]{:S(2)}, u32[]{:S(2)}) collective-permute-start(s16[272,128]{1,0:T(8,128)(2,1)S(1)} %get-tuple-element.9), channel_id=1, source_target_pairs={{0,2},{2,0},{1,3},{3,1},{4,6},{6,4},{5,7},{7,5},{8,10},{10,8},{9,1... | collective-permute-start | bytes 208904 | tf_op jit(solution)/shard_map/ppermute | solution.py:311
  25.7 3.2 %collective-permute-start.2 = (f32[256,128]{1,0:T(8,128)S(1)}, f32[256,128]{1,0:T(8,128)S(1)}, u32[]{:S(2)}, u32[]{:S(2)}) collective-permute-start(f32[256,128]{1,0:T(8,128)S(1)} %shard_map.106.mine_ref), channel_id=1, source_target_pairs={{0,1},{1,0},{2,3},{3,2},{4,5},{5,4},{6,7},{7,6},{8,9},{9,8},{10,11... | collective-permute-start | bytes 393224 | tf_op jit(solution)/shard_map/ppermute | solution.py:313

commit v3 on v2

--- a/solution.py
+++ b/solution.py
@@ -49,8 +49,8 @@
 
 def low_kernel(
     lengths_hbm, policy_hbm, adv_hbm, old_hbm, new_hbm, acts_hbm, cot_hbm, down_hbm, up_hbm,
-    keep_ref, send_ref,
-    x_ref, lengths_ref, policy_ref, adv_ref, old_ref, new_ref, acts_ref, cot_ref, down_ref, up_ref, sems,
+    keep_ref, send_ref, owner_ref, acts_ref, cot_ref,
+    x_ref, lengths_ref, policy_ref, adv_ref, old_ref, new_ref, down_ref, up_ref, sems,
 ):
     tokens, wide_a = acts_ref.shape
     half = tokens // 2
@@ -82,6 +82,11 @@
         total = jnp.full((8, 128), adv_ref[0, s], F32) / jnp.full((8, 128), lengths_ref[0, s], I32).astype(F32)
         owner = jnp.where(inside, policy_ref[0, s], owner)
         factor = jnp.where(inside, total[0:1, :], factor)
+    pos = lax.broadcasted_iota(I32, (POLICIES, tokens), 1)
+    held = jnp.full((POLICIES, tokens), -1, I32)
+    for s in range(SEQS):
+        held = jnp.where((pos >= bounds[s]) & (pos < bounds[s + 1]), policy_ref[0, s], held)
+    owner_ref[...] = held
     ratio = jnp.clip(jnp.exp(new_ref[...] - old_ref[...]), CLIP_LOW, CLIP_HIGH) * ADAPTER_SCALE
     groups = ratio.shape[0]
     ratio = jnp.concatenate([ratio, jnp.zeros((128 - groups, 128), F32)], axis=0).T
@@ -139,18 +144,20 @@
         out_ref[at, :] = sum_ref[at, :] + from_i16(got_ref[at, :]) * scale[b : b + 1]
 
 
-def quantize(values_a, values_b, width_a):
+def quantize(values_a, values_b):
     code_a = code_of(jnp.max(jnp.abs(values_a), axis=1, keepdims=True))
     code_b = code_of(jnp.max(jnp.abs(values_b), axis=1, keepdims=True))
     lane = lax.broadcasted_iota(I32, (values_a.shape[0], 128), 1)
-    codes = jnp.where(lane < 64, code_a, code_b)
+    codes = jnp.where(lane == 0, code_a, code_b)
     inverse = TOP / scale_of(codes)
     q_a = to_i16(values_a * inverse[:, 0:1])
-    q_b = to_i16(values_b * inverse[:, 64:65])
-    return q_a, q_b, codes.astype(I32).astype(I16)
-
-
-def grad_kernel(lengths_ref, policy_ref, mine_ref, other_ref, acts_ref, cot_ref, out_ref, full_ref, fa_ref, fb_ref):
+    q_b = to_i16(values_b * inverse[:, 1:2])
+    return q_a, q_b, codes
+
+
+def grad_kernel(
+    owner_ref, mine_ref, other_ref, acts_ref, cot_ref, out_ref, full_ref, low_ref, left_ref, fa_ref, fb_ref
+):
     tokens, wide_a = acts_ref.shape
     wide_b = cot_ref.shape[1]
     half = tokens // 2
@@ -158,59 +165,83 @@
     full_ref[pl.ds(pl.multiple_of(core * half, half), half), :] = mine_ref[...]
     full_ref[pl.ds(pl.multiple_of((1 - core) * half, half), half), :] = other_ref[...]
     low = full_ref[...].T
-    bounds = starts_of(lengths_ref)
-    pos = lax.broadcasted_iota(I32, (POLICIES * 4, tokens), 1)
-    member = lax.broadcasted_iota(I32, (POLICIES * 4, tokens), 0) // 4
-    owner = jnp.full((POLICIES * 4, tokens), -1, I32)
-    for s in range(SEQS):
-        owner = jnp.where((pos >= bounds[s]) & (pos < bounds[s + 1]), policy_ref[0, s], owner)
-    mask = owner == member
-
-    def wide(rows):
-        groups = []
-        for k in range(4):
-            for d in range(4):
-                first = rows[k * 16 + d * 4 : k * 16 + d * 4 + 4]
-                second = rows[d * 16 + k * 4 : d * 16 + k * 4 + 4]
-                part = jnp.where(core == 0, first, second)
-                part = jnp.concatenate([part] * POLICIES, axis=0)
-                groups.append(jnp.where(mask, part, 0.0))
-        both = jnp.concatenate(groups, axis=0)
-        high = both.astype(BF16)
-        return high, (both - high.astype(F32)).astype(BF16)
-
-    for rows, x_ref, f_ref in ((low[RANK:], acts_ref, fa_ref), (low[:RANK], cot_ref, fb_ref)):
-        high, rest = wide(rows)
-        width = x_ref.shape[1]
-        for c0 in range(0, width, 256):
-            c1 = min(c0 + 256, width)
-            x = x_ref[:, c0:c1]
-            f_ref[:, c0:c1] = jnp.dot(high, x, preferred_element_type=F32) + jnp.dot(
-                rest, x, preferred_element_type=F32
-            )
-    step = out_ref.shape[1]
-    for k in range(4):
-        at = slice(k * step, (k + 1) * step)
-        q_a, q_b, codes = quantize(fa_ref[at, :], fb_ref[at, :], wide_a)
-        out_ref[k, :, :wide_a] = q_a
-        out_ref[k, :, wide_a : wide_a + wide_b] = q_b
-        out_ref[k, :, wide_a + wide_b :] = codes
-
-
-def sum_parts(got_ref, wide_a, wide_b):
+    high = low.astype(BF16).astype(F32)
+    low_ref[0] = high
+    low_ref[1] = low - high
+    mask = owner_ref[...] == lax.broadcasted_iota(I32, (POLICIES, tokens), 0)
+
+    def spread(side, first_rank):
+        for part in range(2):
+            for k in range(4):
+                for d in range(4):
+                    start = first_rank + jnp.where(core == 0, k * 16 + d * 4, d * 16 + k * 4)
+                    at = part * 256 + (k % 2) * 128 + d * 32
+                    rows = []
+                    for i in range(4):
+                        row = low_ref[part, pl.ds(start + i, 1), :]
+                        rows.append(jnp.where(mask, jnp.broadcast_to(row, mask.shape), 0.0))
+                    left_ref[side, k // 2, at : at + 32, :] = jnp.concatenate(rows, axis=0).astype(BF16)
+
+    spread(0, RANK)
+    spread(1, 0)
+    quarter = full_rows(out_ref, wide_a + wide_b)
+    for h in range(2):
+        rows = slice(h * 2 * quarter, (h + 1) * 2 * quarter)
+        for side, x_ref, f_ref in ((0, acts_ref, fa_ref), (1, cot_ref, fb_ref)):
+            left = left_ref[side, h]
+            width = x_ref.shape[1]
+            for c0 in range(0, width, 256):
+                c1 = min(c0 + 256, width)
+                both = jnp.dot(left, x_ref[:, c0:c1], preferred_element_type=F32)
+                f_ref[rows, c0:c1] = both[: 2 * quarter] + both[2 * quarter :]
+        for k in (2 * h, 2 * h + 1):
+            at = slice(k * quarter, (k + 1) * quarter)
+            q_a, q_b, codes = quantize(fa_ref[at, :], fb_ref[at, :])
+            store_columns(out_ref, k, q_a, q_b)
+            out_ref[k, -16:, :] = codes.T[:16].astype(I32).astype(I16)
+
+
+def full_rows(ref, width):
+    return (ref.shape[1] - 16) // (width // 128)
+
+
+def store_columns(out_ref, k, q_a, q_b):
+    rows, at = q_a.shape[0], 0
+    for q in (q_a, q_b):
+        for c in range(0, q.shape[1], 128):
+            out_ref[k, at : at + rows, :] = q[:, c : c + 128]
+            at += rows
+
+
+def sum_parts(scales, parts):
     total_a = total_b = None
-    for k in range(got_ref.shape[0]):
-        scale = scale_of(from_i16(got_ref[k, :, wide_a + wide_b :])) * (1.0 / TOP)
-        a = from_i16(got_ref[k, :, :wide_a]) * scale[:, 0:1]
-        b = from_i16(got_ref[k, :, wide_a : wide_a + wide_b]) * scale[:, 64:65]
+    for (s_a, s_b), (a, b) in zip(scales, parts):
+        a, b = from_i16(a) * s_a, from_i16(b) * s_b
         total_a = a if total_a is None else total_a + a
         total_b = b if total_b is None else total_b + b
     return total_a, total_b
 
 
 def second_kernel(wide_a, wide_b, got_ref, out_ref):
-    total_a, total_b = sum_parts(got_ref, wide_a, wide_b)
-    q_a, q_b, codes = quantize(total_a, total_b, wide_a)
+    rows = full_rows(got_ref, wide_a + wide_b)
+    n_a, n_b = wide_a // 128, wide_b // 128
+    scales = []
+    for k in range(4):
+        codes = from_i16(got_ref[k, -16:, :])
+        codes = scale_of(jnp.concatenate([codes, jnp.zeros((112, 128), F32)], axis=0).T) * (1.0 / TOP)
+        scales.append((codes[:, 0:1], codes[:, 1:2]))
+
+    def column(c):
+        total = None
+        for k in range(4):
+            part = from_i16(got_ref[k, c * rows : (c + 1) * rows, :]) * scales[k][0 if c < n_a else 1]
+            total = part if total is None else total + part
+        return total
+
+    total_a = jnp.concatenate([column(c) for c in range(n_a)], axis=1)
+    total_b = jnp.concatenate([column(c) for c in range(n_a, n_a + n_b)], axis=1)
+    q_a, q_b, codes = quantize(total_a, total_b)
+    codes = codes.astype(I32).astype(I16)
     rows = out_ref.shape[1]
     for k in range(4):
         at = slice(k * rows, (k + 1) * rows)
@@ -219,18 +250,32 @@
         out_ref[k, :, wide_a + wide_b :] = codes[at]
 
 
-def third_kernel(wide_a, wide_b, got_ref, out_ref):
-    total_a, total_b = sum_parts(got_ref, wide_a, wide_b)
+def third_kernel(wide_a, wide_b, got_ref, out_ref, total_ref):
+    parts, scales = [], []
+    for k in range(4):
+        codes = scale_of(from_i16(got_ref[k, :, wide_a + wide_b :])) * (1.0 / TOP)
+        scales.append((codes[:, 0:1], codes[:, 1:2]))
+        parts.append((got_ref[k, :, :wide_a], got_ref[k, :, wide_a : wide_a + wide_b]))
+    total_a, total_b = sum_parts(scales, parts)
+    n_a, n_b = wide_a // 128, wide_b // 128
+    for c in range(n_a):
+        total_ref[c * 32 : (c + 1) * 32, :] = total_a[:, c * 128 : (c + 1) * 128]
+    for c in range(n_b):
+        total_ref[(n_a + c) * 32 : (n_a + c + 1) * 32, :] = total_b[:, c * 128 : (c + 1) * 128]
+
+    def code_for(parts):
+        most = jnp.abs(parts[0])
+        for part in parts[1:]:
+            most = jnp.maximum(most, jnp.abs(part))
+        return code_of(jnp.max(jnp.max(most, axis=0, keepdims=True), axis=1, keepdims=True))
+
     for p in range(POLICIES):
-        a = total_a[p * 4 : (p + 1) * 4]
-        b = total_b[p * 4 : (p + 1) * 4]
-        code_a = code_of(jnp.max(jnp.abs(a)).reshape(1, 1))
-        code_b = code_of(jnp.max(jnp.abs(b)).reshape(1, 1))
-        pieces = [a[:, c : c + 128] * (TOP / scale_of(code_a)) for c in range(0, wide_a, 128)]
-        pieces += [b[:, c : c + 128] * (TOP / scale_of(code_b)) for c in range(0, wide_b, 128)]
-        pieces.append(jnp.broadcast_to(code_a, (4, 128)))
-        pieces.append(jnp.broadcast_to(code_b, (4, 128)))
-        pieces.append(jnp.zeros((4, 128), F32))
+        parts = [total_ref[pl.ds(c * 32 + p, 4, stride=POLICIES), :] for c in range(n_a + n_b)]
+        code_a, code_b = code_for(parts[:n_a]), code_for(parts[n_a:])
+        pieces = [part * (TOP / scale_of(code_a)) for part in parts[:n_a]]
+        pieces += [part * (TOP / scale_of(code_b)) for part in parts[n_a:]]
+        row = lax.broadcasted_iota(I32, (4, 128), 0)
+        pieces.append(jnp.where(row == 0, code_a, code_b))
         out_ref[p] = to_i16(jnp.concatenate(pieces, axis=0))
 
 
@@ -241,7 +286,7 @@
         values = from_i16(got_ref[k])
         at = 4 * (n_a + n_b)
         s_a = scale_of(values[at : at + 1]) * (1.0 / TOP)
-        s_b = scale_of(values[at + 4 : at + 5]) * (1.0 / TOP)
+        s_b = scale_of(values[at + 1 : at + 2]) * (1.0 / TOP)
         row = lax.broadcasted_iota(I32, values.shape, 0)
         values = values * jnp.where(row < 4 * n_a, s_a, s_b)
         total = values if total is None else total + values
@@ -288,9 +333,9 @@
     core_pairs = [(0, 1), (1, 0), (2, 3), (3, 2)]
     far_pairs = [(0, 2), (2, 0), (1, 3), (3, 1)]
     lines = (tokens // 128, 128)
-    keep, send = call(
+    keep, send, owner, acts, cot = call(
         low_kernel,
-        [((half, 128), F32)] * 2,
+        [((half, 128), F32)] * 2 + [((POLICIES, tokens), I32), (acts.shape, BF16), (cot.shape, BF16)],
         [HBM] * 9,
         [
             VMEM((tokens, 128), F32),
@@ -299,8 +344,6 @@
             SMEM(advantages.shape, F32),
             VMEM(lines, F32),
             VMEM(lines, F32),
-            VMEM(acts.shape, BF16),
-            VMEM(cot.shape, BF16),
             VMEM(down.shape, BF16),
             VMEM(up.shape, BF16),
             pltpu.SemaphoreType.DMA((11,)),
@@ -315,18 +358,24 @@
     width = wide_a + wide_b + 128
     (pieces,) = call(
         grad_kernel,
-        [((4, rows // 4, width), I16)],
-        [SMEM] * 2 + [VMEM] * 4,
-        [VMEM((tokens, 128), F32), VMEM((rows, wide_a), F32), VMEM((rows, wide_b), F32)],
-    )(lengths, policy, mine, other, acts, cot)
+        [((4, rows // 4 * (wide_a + wide_b) // 128 + 16, 128), I16)],
+        [VMEM] * 5,
+        [
+            VMEM((tokens, 128), F32),
+            VMEM((2, 2 * RANK, tokens), F32),
+            VMEM((2, 2, rows, tokens), BF16),
+            VMEM((rows, wide_a), F32),
+            VMEM((rows, wide_b), F32),
+        ],
+    )(owner, mine, other, acts, cot)
     got = lax.all_to_all(pieces, BOTH, 0, 0, tiled=True, axis_index_groups=first)
     (pieces,) = call(
         functools.partial(second_kernel, wide_a, wide_b), [((4, rows // 16, width), I16)], [VMEM]
     )(got)
     got = lax.all_to_all(pieces, BOTH, 0, 0, tiled=True, axis_index_groups=second)
-    deep = 4 * (wide_a + wide_b) // 128 + 12
+    deep = 4 * (wide_a + wide_b) // 128 + 4
     (pieces,) = call(
-        functools.partial(third_kernel, wide_a, wide_b), [((POLICIES, deep, 128), I16)], [VMEM]
+        functools.partial(third_kernel, wide_a, wide_b), [((POLICIES, deep, 128), I16)], [VMEM], [VMEM((rows // 16 * (wide_a + wide_b) // 128, 128), F32)]
     )(got)
     got = lax.all_to_all(pieces, BOTH, 0, 0, tiled=True, axis_index_groups=third)
     return tuple(

time: 87 us -> 85.5 us (0.983)
  no operation moved by 1% of the time
where the time goes in v3:
time: 85.5 us; the launch traced here: 85.2 us
  blocking collectives  52 us (61%)
  starting transfers between devices  19.6 us (23%)
  Pallas kernels  7.52 us (9%)
  waiting for transfers between devices  5.4 us (6%)
    all_to_all x1, blocking collectives, shards(): lax.all_to_all(pieces, BOTH, 0, 0, tiled=True, axis_index_groups=third)  22.3 us
    all_to_all x1, blocking collectives, shards(): lax.all_to_all(pieces, BOTH, 0, 0, tiled=True, axis_index_groups=first)  17.8 us
    ppermute x1, starting transfers between devices, shards(): far = lax.ppermute(packed, 'mp', far_pairs)  15.7 us
    all_to_all x1, blocking collectives, shards(): lax.all_to_all(pieces, BOTH, 0, 0, tiled=True, axis_index_groups=second)  11.9 us
    pallas_call x1, Pallas kernels, shards(): call(low_kernel, [((half, 128), F32)] * 2 + [((POLICIES, tokens), I32), (...  3.01 us
    ppermute x1, waiting for transfers between devices, shards(): far = lax.ppermute(packed, 'mp', far_pairs)  2.78 us
    pallas_call x1, Pallas kernels, shards(): call(grad_kernel, [((4, rows // 4 * (wide_a + wide_b) // 128 + 16, 128),...  2.68 us
    ppermute x1, starting transfers between devices, shards(): got = lax.ppermute(send, 'mp', core_pairs)  1.92 us
  transfers between devices with their start and end apart: 3, of which 3 were waited for; matrix products, arithmetic and copies ran while one was open for 0% of the time, Pallas kernels for 0%

profile of v3, /device:TPU:2, one launch (start us, length us, event | category | flops | bytes accessed | tf_op | source)
XLA Modules:
  0.0 85.2 jit_solution(1384730318091725528)
XLA Ops:
  0.6 3.0 %shard_map.104 = (f32[256,128]{1,0:T(8,128)S(1)}, f32[256,128]{1,0:T(8,128)S(1)}, s32[8,512]{1,0:T(8,128)S(1)}, bf16[512,1152]{1,0:T(8,128)(2,1)S(1)}, bf16[512,512]{1,0:T(8,128)(2,1)S(1)}) custom-call(s32[1,8]{1,0:T(1,128)} %lengths_hbm.1, s32[1,8]{1,0:T(1,128)} %policy_hbm.1, f32[1,8]{1,0:T(1,128)} %adv_hbm.1, f32[4,128]{1,0:T(4,128)} %bitcast.2, ...), custom_call_target="tpu_custom_call" | custom-call | tf_op jit(solution)/shard_map/pallas_call | solution.py:336
  3.7 1.9 %collective-permute-start = (f32[256,128]{1,0:T(8,128)S(1)}, f32[256,128]{1,0:T(8,128)S(1)}, u32[]{:S(2)}, u32[]{:S(2)}) collective-permute-start(f32[256,128]{1,0:T(8,128)S(1)} %get-tuple-element.11), channel_id=1, source_target_pairs={{0,1},{1,0},{2,3},{3,2},{4,5},{5,4},{6,7},{7,6},{8,9},{9,8},{10,11... | collective-permute-start | bytes 393224 | tf_op jit(solution)/shard_map/ppermute | solution.py:352
  5.6 1.3 %collective-permute-done.got_ref = f32[256,128]{1,0:T(8,128)S(1)} collective-permute-done((f32[256,128]{1,0:T(8,128)S(1)}, f32[256,128]{1,0:T(8,128)S(1)}, u32[]{:S(2)}, u32[]{:S(2)}) %collective-permute-start) | collective-permute-done | bytes 131104 | tf_op jit(solution)/shard_map/ppermute | solution.py:352
  6.9 0.1 shard_map.105
  7.0 15.7 %collective-permute-start.1 = (s16[272,128]{1,0:T(8,128)(2,1)S(1)}, s16[272,128]{1,0:T(8,128)(2,1)S(1)}, u32[]{:S(2)}, u32[]{:S(2)}) collective-permute-start(s16[272,128]{1,0:T(8,128)(2,1)S(1)} %get-tuple-element.13), channel_id=1, source_target_pairs={{0,2},{2,0},{1,3},{3,1},{4,6},{6,4},{5,7},{7,5},{8,10},{10,8},{9,1... | collective-permute-start | bytes 208904 | tf_op jit(solution)/shard_map/ppermute | solution.py:354
  22.7 2.8 %collective-permute-done.1.got_ref = s16[272,128]{1,0:T(8,128)(2,1)S(1)} collective-permute-done((s16[272,128]{1,0:T(8,128)(2,1)S(1)}, s16[272,128]{1,0:T(8,128)(2,1)S(1)}, u32[]{:S(2)}, u32[]{:S(2)}) %collective-permute-start.1) | collective-permute-done | bytes 69664 | tf_op jit(solution)/shard_map/ppermute | solution.py:354
  25.5 1.9 %collective-permute-start.2 = (f32[256,128]{1,0:T(8,128)S(1)}, f32[256,128]{1,0:T(8,128)S(1)}, u32[]{:S(2)}, u32[]{:S(2)}) collective-permute-start(f32[256,128]{1,0:T(8,128)S(1)} %shard_map.106.mine_ref), channel_id=1, source_target_pairs={{0,1},{1,0},{2,3},{3,2},{4,5},{5,4},{6,7},{7,6},{8,9},{9,8},{10,11... | collective-permute-start | bytes 393224 | tf_op jit(solution)/shard_map/ppermute | solution.py:356
  27.4 1.3 %collective-permute-done.2.other_ref = f32[256,128]{1,0:T(8,128)S(1)} collective-permute-done((f32[256,128]{1,0:T(8,128)S(1)}, f32[256,128]{1,0:T(8,128)S(1)}, u32[]{:S(2)}, u32[]{:S(2)}) %collective-permute-start.2) | collective-permute-done | bytes 131104 | tf_op jit(solution)/shard_map/ppermute | solution.py:356
  28.7 2.7 %shard_map.107 = s16[4,1680,128]{2,1,0:T(8,128)(2,1)S(1)} custom-call(s32[8,512]{1,0:T(8,128)S(1)} %get-tuple-element.9.owner_ref, f32[256,128]{1,0:T(8,128)S(1)} %shard_map.106.mine_ref, f32[256,128]{1,0:T(8,128)S(1)} %collective-permute-done.2.other_ref, bf16[512,1152]{1,0:T(8,128)(2,1)S(1)} %get-tuple-element.14.acts_ref, ...), custom_call_target="tpu_custom_call" | custom-call | tf_op jit(solution)/shard_map/pallas_call | solution.py:359
  31.4 17.8 %all_to_all.15.got_ref = s16[4,1680,128]{2,1,0:T(8,128)(2,1)S(1)} all-to-all(s16[4,1680,128]{2,1,0:T(8,128)(2,1)S(1)} %shard_map.107), channel_id=1, replica_groups={{0,16,32,48},{1,5,9,13},{4,20,36,52},{17,21,25,29},{8,24,40,56},{33,37,..., dimensions={0} | all-to-all | bytes 3440640 | tf_op jit(solution)/shard_map/all_to_all | solution.py:371
  49.2 0.8 shard_map.108
  50.0 11.9 %all_to_all.16.got_ref = s16[4,32,1792]{2,1,0:T(8,128)(2,1)S(1)} all-to-all(s16[4,32,1792]{2,1,0:T(8,128)(2,1)S(1)} %shard_map.108), channel_id=1, replica_groups={{0,4,8,12},{1,17,33,49},{16,20,24,28},{5,21,37,53},{32,36,40,44},{9,25,..., dimensions={0} | all-to-all | bytes 917504 | tf_op jit(solution)/shard_map/all_to_all | solution.py:375
  61.9 0.3 shard_map.109
  62.2 22.3 %all_to_all.17.got_ref = s16[8,56,128]{2,1,0:T(8,128)(2,1)S(1)} all-to-all(s16[8,56,128]{2,1,0:T(8,128)(2,1)S(1)} %shard_map.109), channel_id=1, replica_groups={{0,64,128,192,256,320,384,448},{1,65,129,193,257,321,385,449},{2,66,130..., dimensions={0} | all-to-all | bytes 229376 | tf_op jit(solution)/shard_map/all_to_all | solution.py:380
  84.5 0.6 shard_map.110
  (1 shorter events, 0.0 us)
Async XLA Ops:
  3.7 3.2 %collective-permute-start = (f32[256,128]{1,0:T(8,128)S(1)}, f32[256,128]{1,0:T(8,128)S(1)}, u32[]{:S(2)}, u32[]{:S(2)}) collective-permute-start(f32[256,128]{1,0:T(8,128)S(1)} %get-tuple-element.11), channel_id=1, source_target_pairs={{0,1},{1,0},{2,3},{3,2},{4,5},{5,4},{6,7},{7,6},{8,9},{9,8},{10,11... | collective-permute-start | bytes 393224 | tf_op jit(solution)/shard_map/ppermute | solution.py:352
  7.0 18.5 %collective-permute-start.1 = (s16[272,128]{1,0:T(8,128)(2,1)S(1)}, s16[272,128]{1,0:T(8,128)(2,1)S(1)}, u32[]{:S(2)}, u32[]{:S(2)}) collective-permute-start(s16[272,128]{1,0:T(8,128)(2,1)S(1)} %get-tuple-element.13), channel_id=1, source_target_pairs={{0,2},{2,0},{1,3},{3,1},{4,6},{6,4},{5,7},{7,5},{8,10},{10,8},{9,1... | collective-permute-start | bytes 208904 | tf_op jit(solution)/shard_map/ppermute | solution.py:354
  25.5 3.2 %collective-permute-start.2 = (f32[256,128]{1,0:T(8,128)S(1)}, f32[256,128]{1,0:T(8,128)S(1)}, u32[]{:S(2)}, u32[]{:S(2)}) collective-permute-start(f32[256,128]{1,0:T(8,128)S(1)} %shard_map.106.mine_ref), channel_id=1, source_target_pairs={{0,1},{1,0},{2,3},{3,2},{4,5},{5,4},{6,7},{7,6},{8,9},{9,8},{10,11... | collective-permute-start | bytes 393224 | tf_op jit(solution)/shard_map/ppermute | solution.py:356

commit v4 on v3

--- a/solution.py
+++ b/solution.py
@@ -118,6 +118,7 @@
 
 
 BLOCKS = 4
+NEAR = 4
 
 
 def pack_kernel(keep_ref, got_ref, sum_ref, out_ref):
@@ -269,27 +270,57 @@
             most = jnp.maximum(most, jnp.abs(part))
         return code_of(jnp.max(jnp.max(most, axis=0, keepdims=True), axis=1, keepdims=True))
 
-    for p in range(POLICIES):
+    def piece_of(p):
         parts = [total_ref[pl.ds(c * 32 + p, 4, stride=POLICIES), :] for c in range(n_a + n_b)]
         code_a, code_b = code_for(parts[:n_a]), code_for(parts[n_a:])
         pieces = [part * (TOP / scale_of(code_a)) for part in parts[:n_a]]
         pieces += [part * (TOP / scale_of(code_b)) for part in parts[n_a:]]
         row = lax.broadcasted_iota(I32, (4, 128), 0)
-        pieces.append(jnp.where(row == 0, code_a, code_b))
-        out_ref[p] = to_i16(jnp.concatenate(pieces, axis=0))
-
-
-def last_kernel(wide_a, wide_b, got_ref, a_ref, b_ref):
+        return pieces + [jnp.where(row == 0, code_a, code_b)]
+
+    for m in range(NEAR):
+        pieces = []
+        for p in range(m, POLICIES, NEAR):
+            pieces += piece_of(p)
+        out_ref[m] = to_i16(jnp.concatenate(pieces, axis=0))
+
+
+def open_piece(values, n_a, n_b):
+    at = 4 * (n_a + n_b)
+    s_a = scale_of(values[at : at + 1]) * (1.0 / TOP)
+    s_b = scale_of(values[at + 1 : at + 2]) * (1.0 / TOP)
+    row = lax.broadcasted_iota(I32, values.shape, 0)
+    return values * jnp.where(row < 4 * n_a, s_a, s_b)
+
+
+def fourth_kernel(wide_a, wide_b, got_ref, mine_ref, out_ref):
     n_a, n_b = wide_a // 128, wide_b // 128
-    total = None
-    for k in range(POLICIES):
+    deep = 4 * (n_a + n_b) + 4
+    low = high = None
+    for k in range(NEAR):
         values = from_i16(got_ref[k])
-        at = 4 * (n_a + n_b)
-        s_a = scale_of(values[at : at + 1]) * (1.0 / TOP)
-        s_b = scale_of(values[at + 1 : at + 2]) * (1.0 / TOP)
-        row = lax.broadcasted_iota(I32, values.shape, 0)
-        values = values * jnp.where(row < 4 * n_a, s_a, s_b)
-        total = values if total is None else total + values
+        first, second = open_piece(values[:deep], n_a, n_b), open_piece(values[deep:], n_a, n_b)
+        low = first if low is None else low + first
+        high = second if high is None else high + second
+    upper = lax.axis_index("dp") // 16 >= NEAR
+    mine_ref[...] = jnp.where(upper, high, low)
+    other = jnp.where(upper, low, high)
+    row = lax.broadcasted_iota(I32, other.shape, 0)
+
+    def code_for(first, last):
+        most = jnp.where((row >= first) & (row < last), jnp.abs(other), 0.0)
+        return code_of(jnp.max(jnp.max(most, axis=0, keepdims=True), axis=1, keepdims=True))
+
+    code_a, code_b = code_for(0, 4 * n_a), code_for(4 * n_a, deep - 4)
+    values = other * jnp.where(row < 4 * n_a, TOP / scale_of(code_a), TOP / scale_of(code_b))
+    values = jnp.where(row < deep - 4, values, jnp.where(row == deep - 4, code_a, code_b))
+    out_ref[...] = to_i16(jnp.concatenate([values, jnp.zeros((8, 128), F32)], axis=0))
+
+
+def last_kernel(wide_a, wide_b, mine_ref, got_ref, a_ref, b_ref):
+    n_a, n_b = wide_a // 128, wide_b // 128
+    values = from_i16(got_ref[...])[: mine_ref.shape[0]]
+    total = mine_ref[...] + open_piece(values, n_a, n_b)
     for c in range(n_a):
         a_ref[:, c * 128 : (c + 1) * 128] = total[c * 4 : (c + 1) * 4]
     for c in range(n_b):
@@ -321,7 +352,14 @@
                 first.append(index[z, k, :, h, 1].tolist())
                 second.append(index[z, k, :, h, 0].tolist())
                 second.append(index[z, :, k, h, 1].tolist())
-    third = [index[:, x, y, h, c].tolist() for x in range(4) for y in range(4) for h in range(2) for c in range(2)]
+    third = [
+        index[z : z + NEAR, x, y, h, c].tolist()
+        for z in (0, NEAR)
+        for x in range(4)
+        for y in range(4)
+        for h in range(2)
+        for c in range(2)
+    ]
     return first, second, third
 
 
@@ -375,13 +413,20 @@
     got = lax.all_to_all(pieces, BOTH, 0, 0, tiled=True, axis_index_groups=second)
     deep = 4 * (wide_a + wide_b) // 128 + 4
     (pieces,) = call(
-        functools.partial(third_kernel, wide_a, wide_b), [((POLICIES, deep, 128), I16)], [VMEM], [VMEM((rows // 16 * (wide_a + wide_b) // 128, 128), F32)]
+        functools.partial(third_kernel, wide_a, wide_b), [((NEAR, 2 * deep, 128), I16)], [VMEM], [VMEM((rows // 16 * (wide_a + wide_b) // 128, 128), F32)]
     )(got)
     got = lax.all_to_all(pieces, BOTH, 0, 0, tiled=True, axis_index_groups=third)
+    part, packed = call(
+        functools.partial(fourth_kernel, wide_a, wide_b),
+        [((deep, 128), F32), ((deep + 8, 128), I16)],
+        [VMEM],
+    )(got)
+    count = lax.axis_size("dp")
+    got = lax.ppermute(packed, "dp", [(i, (i + count // 2) % count) for i in range(count)])
     return tuple(
         call(
-            functools.partial(last_kernel, wide_a, wide_b), [((4, wide_a), F32), ((4, wide_b), F32)], [VMEM]
-        )(got)
+            functools.partial(last_kernel, wide_a, wide_b), [((4, wide_a), F32), ((4, wide_b), F32)], [VMEM] * 2
+        )(part, got)
     )
 
 

time: 85.5 us -> 84.8 us (level)
  the two profiles are of different devices: /device:TPU:2 before, /device:TPU:32 now
where the time goes in v4:
time: 84.8 us; the launch traced here: 84.5 us
  blocking collectives  39.2 us (46%)
  starting transfers between devices  28.3 us (33%)
  waiting for transfers between devices  8.54 us (10%)
  Pallas kernels  7.64 us (9%)
    all_to_all x1, blocking collectives, shards(): lax.all_to_all(pieces, BOTH, 0, 0, tiled=True, axis_index_groups=first)  18.6 us
    ppermute x1, starting transfers between devices, shards(): far = lax.ppermute(packed, 'mp', far_pairs)  14.8 us
    all_to_all x1, blocking collectives, shards(): lax.all_to_all(pieces, BOTH, 0, 0, tiled=True, axis_index_groups=second)  12 us
    ppermute x1, starting transfers between devices, shards(): lax.ppermute(packed, 'dp', [(i, (i + count // 2) % count) for i in range(...  9.67 us
    all_to_all x1, blocking collectives, shards(): lax.all_to_all(pieces, BOTH, 0, 0, tiled=True, axis_index_groups=third)  8.66 us
    ppermute x1, waiting for transfers between devices, shards(): far = lax.ppermute(packed, 'mp', far_pairs)  4.16 us
    pallas_call x1, Pallas kernels, shards(): call(low_kernel, [((half, 128), F32)] * 2 + [((POLICIES, tokens), I32), (...  3.01 us
    pallas_call x1, Pallas kernels, shards(): call(grad_kernel, [((4, rows // 4 * (wide_a + wide_b) // 128 + 16, 128),...  2.68 us
  transfers between devices with their start and end apart: 4, of which 4 were waited for; matrix products, arithmetic and copies ran while one was open for 0% of the time, Pallas kernels for 0%

profile of v4, /device:TPU:32, one launch (start us, length us, event | category | flops | bytes accessed | tf_op | source)
XLA Modules:
  0.0 84.5 jit_solution(1606750463067759019)
XLA Ops:
  0.6 3.0 %shard_map.104 = (f32[256,128]{1,0:T(8,128)S(1)}, f32[256,128]{1,0:T(8,128)S(1)}, s32[8,512]{1,0:T(8,128)S(1)}, bf16[512,1152]{1,0:T(8,128)(2,1)S(1)}, bf16[512,512]{1,0:T(8,128)(2,1)S(1)}) custom-call(s32[1,8]{1,0:T(1,128)} %lengths_hbm.1, s32[1,8]{1,0:T(1,128)} %policy_hbm.1, f32[1,8]{1,0:T(1,128)} %adv_hbm.1, f32[4,128]{1,0:T(4,128)} %bitcast.2, ...), custom_call_target="tpu_custom_call" | custom-call | tf_op jit(solution)/shard_map/pallas_call | solution.py:374
  3.7 1.9 %collective-permute-start = (f32[256,128]{1,0:T(8,128)S(1)}, f32[256,128]{1,0:T(8,128)S(1)}, u32[]{:S(2)}, u32[]{:S(2)}) collective-permute-start(f32[256,128]{1,0:T(8,128)S(1)} %get-tuple-element.13), channel_id=1, source_target_pairs={{0,1},{1,0},{2,3},{3,2},{4,5},{5,4},{6,7},{7,6},{8,9},{9,8},{10,11... | collective-permute-start | bytes 393224 | tf_op jit(solution)/shard_map/ppermute | solution.py:390
  5.6 1.3 %collective-permute-done.got_ref = f32[256,128]{1,0:T(8,128)S(1)} collective-permute-done((f32[256,128]{1,0:T(8,128)S(1)}, f32[256,128]{1,0:T(8,128)S(1)}, u32[]{:S(2)}, u32[]{:S(2)}) %collective-permute-start) | collective-permute-done | bytes 131104 | tf_op jit(solution)/shard_map/ppermute | solution.py:390
  6.9 0.1 shard_map.105
  7.0 14.8 %collective-permute-start.1 = (s16[272,128]{1,0:T(8,128)(2,1)S(1)}, s16[272,128]{1,0:T(8,128)(2,1)S(1)}, u32[]{:S(2)}, u32[]{:S(2)}) collective-permute-start(s16[272,128]{1,0:T(8,128)(2,1)S(1)} %get-tuple-element.15), channel_id=1, source_target_pairs={{0,2},{2,0},{1,3},{3,1},{4,6},{6,4},{5,7},{7,5},{8,10},{10,8},{9,1... | collective-permute-start | bytes 208904 | tf_op jit(solution)/shard_map/ppermute | solution.py:392
  21.8 4.2 %collective-permute-done.1.got_ref = s16[272,128]{1,0:T(8,128)(2,1)S(1)} collective-permute-done((s16[272,128]{1,0:T(8,128)(2,1)S(1)}, s16[272,128]{1,0:T(8,128)(2,1)S(1)}, u32[]{:S(2)}, u32[]{:S(2)}) %collective-permute-start.1) | collective-permute-done | bytes 69664 | tf_op jit(solution)/shard_map/ppermute | solution.py:392
  26.0 1.9 %collective-permute-start.2 = (f32[256,128]{1,0:T(8,128)S(1)}, f32[256,128]{1,0:T(8,128)S(1)}, u32[]{:S(2)}, u32[]{:S(2)}) collective-permute-start(f32[256,128]{1,0:T(8,128)S(1)} %shard_map.106.mine_ref), channel_id=1, source_target_pairs={{0,1},{1,0},{2,3},{3,2},{4,5},{5,4},{6,7},{7,6},{8,9},{9,8},{10,11... | collective-permute-start | bytes 393224 | tf_op jit(solution)/shard_map/ppermute | solution.py:394
  27.9 1.3 %collective-permute-done.2.other_ref = f32[256,128]{1,0:T(8,128)S(1)} collective-permute-done((f32[256,128]{1,0:T(8,128)S(1)}, f32[256,128]{1,0:T(8,128)S(1)}, u32[]{:S(2)}, u32[]{:S(2)}) %collective-permute-start.2) | collective-permute-done | bytes 131104 | tf_op jit(solution)/shard_map/ppermute | solution.py:394
  29.2 2.7 %shard_map.107 = s16[4,1680,128]{2,1,0:T(8,128)(2,1)S(1)} custom-call(s32[8,512]{1,0:T(8,128)S(1)} %get-tuple-element.11.owner_ref, f32[256,128]{1,0:T(8,128)S(1)} %shard_map.106.mine_ref, f32[256,128]{1,0:T(8,128)S(1)} %collective-permute-done.2.other_ref, bf16[512,1152]{1,0:T(8,128)(2,1)S(1)} %get-tuple-element.16.acts_ref, ...), custom_call_target="tpu_custom_call" | custom-call | tf_op jit(solution)/shard_map/pallas_call | solution.py:397
  31.9 18.6 %all_to_all.15.got_ref = s16[4,1680,128]{2,1,0:T(8,128)(2,1)S(1)} all-to-all(s16[4,1680,128]{2,1,0:T(8,128)(2,1)S(1)} %shard_map.107), channel_id=1, replica_groups={{0,16,32,48},{1,5,9,13},{4,20,36,52},{17,21,25,29},{8,24,40,56},{33,37,..., dimensions={0} | all-to-all | bytes 3440640 | tf_op jit(solution)/shard_map/all_to_all | solution.py:409
  50.5 0.8 shard_map.108
  51.3 12.0 %all_to_all.16.got_ref = s16[4,32,1792]{2,1,0:T(8,128)(2,1)S(1)} all-to-all(s16[4,32,1792]{2,1,0:T(8,128)(2,1)S(1)} %shard_map.108), channel_id=1, replica_groups={{0,4,8,12},{1,17,33,49},{16,20,24,28},{5,21,37,53},{32,36,40,44},{9,25,..., dimensions={0} | all-to-all | bytes 917504 | tf_op jit(solution)/shard_map/all_to_all | solution.py:413
  63.3 0.3 shard_map.109
  63.6 8.7 %all_to_all.17.got_ref = s16[4,112,128]{2,1,0:T(8,128)(2,1)S(1)} all-to-all(s16[4,112,128]{2,1,0:T(8,128)(2,1)S(1)} %shard_map.109), channel_id=1, replica_groups={{0,64,128,192},{1,65,129,193},{2,66,130,194},{3,67,131,195},{4,68,132,1..., dimensions={0} | all-to-all | bytes 229376 | tf_op jit(solution)/shard_map/all_to_all | solution.py:418
  72.3 0.1 shard_map.110
  72.4 9.7 %collective-permute-start.3 = (s16[64,128]{1,0:T(8,128)(2,1)S(1)}, s16[64,128]{1,0:T(8,128)(2,1)S(1)}, u32[]{:S(2)}, u32[]{:S(2)}) collective-permute-start(s16[64,128]{1,0:T(8,128)(2,1)S(1)} %get-tuple-element.19), channel_id=1, source_target_pairs={{0,256},{4,260},{8,264},{12,268},{16,272},{20,276},{24,280},{28,28... | collective-permute-start | bytes 49160 | tf_op jit(solution)/shard_map/ppermute | solution.py:425
  82.1 1.8 %collective-permute-done.3.got_ref = s16[64,128]{1,0:T(8,128)(2,1)S(1)} collective-permute-done((s16[64,128]{1,0:T(8,128)(2,1)S(1)}, s16[64,128]{1,0:T(8,128)(2,1)S(1)}, u32[]{:S(2)}, u32[]{:S(2)}) %collective-permute-start.3) | collective-permute-done | bytes 16416 | tf_op jit(solution)/shard_map/ppermute | solution.py:425
  83.8 0.6 shard_map.111
  (1 shorter events, 0.0 us)
Async XLA Ops:
  3.7 3.2 %collective-permute-start = (f32[256,128]{1,0:T(8,128)S(1)}, f32[256,128]{1,0:T(8,128)S(1)}, u32[]{:S(2)}, u32[]{:S(2)}) collective-permute-start(f32[256,128]{1,0:T(8,128)S(1)} %get-tuple-element.13), channel_id=1, source_target_pairs={{0,1},{1,0},{2,3},{3,2},{4,5},{5,4},{6,7},{7,6},{8,9},{9,8},{10,11... | collective-permute-start | bytes 393224 | tf_op jit(solution)/shard_map/ppermute | solution.py:390
  7.0 19.0 %collective-permute-start.1 = (s16[272,128]{1,0:T(8,128)(2,1)S(1)}, s16[272,128]{1,0:T(8,128)(2,1)S(1)}, u32[]{:S(2)}, u32[]{:S(2)}) collective-permute-start(s16[272,128]{1,0:T(8,128)(2,1)S(1)} %get-tuple-element.15), channel_id=1, source_target_pairs={{0,2},{2,0},{1,3},{3,1},{4,6},{6,4},{5,7},{7,5},{8,10},{10,8},{9,1... | collective-permute-start | bytes 208904 | tf_op jit(solution)/shard_map/ppermute | solution.py:392
  26.0 3.2 %collective-permute-start.2 = (f32[256,128]{1,0:T(8,128)S(1)}, f32[256,128]{1,0:T(8,128)S(1)}, u32[]{:S(2)}, u32[]{:S(2)}) collective-permute-start(f32[256,128]{1,0:T(8,128)S(1)} %shard_map.106.mine_ref), channel_id=1, source_target_pairs={{0,1},{1,0},{2,3},{3,2},{4,5},{5,4},{6,7},{7,6},{8,9},{9,8},{10,11... | collective-permute-start | bytes 393224 | tf_op jit(solution)/shard_map/ppermute | solution.py:394
  72.4 11.4 %collective-permute-start.3 = (s16[64,128]{1,0:T(8,128)(2,1)S(1)}, s16[64,128]{1,0:T(8,128)(2,1)S(1)}, u32[]{:S(2)}, u32[]{:S(2)}) collective-permute-start(s16[64,128]{1,0:T(8,128)(2,1)S(1)} %get-tuple-element.19), channel_id=1, source_target_pairs={{0,256},{4,260},{8,264},{12,268},{16,272},{20,276},{24,280},{28,28... | collective-permute-start | bytes 49160 | tf_op jit(solution)/shard_map/ppermute | solution.py:425

commit v5 on v4

--- a/solution.py
+++ b/solution.py
@@ -156,22 +156,16 @@
     return q_a, q_b, codes
 
 
-def grad_kernel(
-    owner_ref, mine_ref, other_ref, acts_ref, cot_ref, out_ref, full_ref, low_ref, left_ref, fa_ref, fb_ref
-):
-    tokens, wide_a = acts_ref.shape
-    wide_b = cot_ref.shape[1]
-    half = tokens // 2
+def half_gradients(other, owner_ref, half_ref, acts_ref, cot_ref, low_ref, left_ref, store):
+    half = half_ref.shape[0]
     core = lax.rem(lax.axis_index("mp"), 2)
-    full_ref[pl.ds(pl.multiple_of(core * half, half), half), :] = mine_ref[...]
-    full_ref[pl.ds(pl.multiple_of((1 - core) * half, half), half), :] = other_ref[...]
-    low = full_ref[...].T
+    tokens = pl.ds(pl.multiple_of((1 - core if other else core) * half, half), half)
+    low = half_ref[...].T
     high = low.astype(BF16).astype(F32)
     low_ref[0] = high
     low_ref[1] = low - high
-    mask = owner_ref[...] == lax.broadcasted_iota(I32, (POLICIES, tokens), 0)
-
-    def spread(side, first_rank):
+    mask = owner_ref[:, tokens] == lax.broadcasted_iota(I32, (POLICIES, half), 0)
+    for side, first_rank in ((0, RANK), (1, 0)):
         for part in range(2):
             for k in range(4):
                 for d in range(4):
@@ -182,22 +176,38 @@
                         row = low_ref[part, pl.ds(start + i, 1), :]
                         rows.append(jnp.where(mask, jnp.broadcast_to(row, mask.shape), 0.0))
                     left_ref[side, k // 2, at : at + 32, :] = jnp.concatenate(rows, axis=0).astype(BF16)
-
-    spread(0, RANK)
-    spread(1, 0)
-    quarter = full_rows(out_ref, wide_a + wide_b)
     for h in range(2):
-        rows = slice(h * 2 * quarter, (h + 1) * 2 * quarter)
-        for side, x_ref, f_ref in ((0, acts_ref, fa_ref), (1, cot_ref, fb_ref)):
+        rows, at = slice(h * 256, (h + 1) * 256), 0
+        for side, x_ref in ((0, acts_ref), (1, cot_ref)):
             left = left_ref[side, h]
             width = x_ref.shape[1]
             for c0 in range(0, width, 256):
                 c1 = min(c0 + 256, width)
-                both = jnp.dot(left, x_ref[:, c0:c1], preferred_element_type=F32)
-                f_ref[rows, c0:c1] = both[: 2 * quarter] + both[2 * quarter :]
+                both = jnp.dot(left, x_ref[tokens, c0:c1], preferred_element_type=F32)
+                store(rows, slice(at + c0, at + c1), both[:256] + both[256:])
+            at += width
+        yield h
+
+
+def own_kernel(owner_ref, half_ref, acts_ref, cot_ref, sum_ref, low_ref, left_ref):
+    def store(rows, columns, values):
+        sum_ref[rows, columns] = values
+
+    for _ in half_gradients(False, owner_ref, half_ref, acts_ref, cot_ref, low_ref, left_ref, store):
+        pass
+
+
+def grad_kernel(owner_ref, half_ref, acts_ref, cot_ref, sum_ref, out_ref, low_ref, left_ref, f_ref):
+    wide_a, wide_b = acts_ref.shape[1], cot_ref.shape[1]
+    quarter = full_rows(out_ref, wide_a + wide_b)
+
+    def store(rows, columns, values):
+        f_ref[rows, columns] = values + sum_ref[rows, columns]
+
+    for h in half_gradients(True, owner_ref, half_ref, acts_ref, cot_ref, low_ref, left_ref, store):
         for k in (2 * h, 2 * h + 1):
             at = slice(k * quarter, (k + 1) * quarter)
-            q_a, q_b, codes = quantize(fa_ref[at, :], fb_ref[at, :])
+            q_a, q_b, codes = quantize(f_ref[at, :wide_a], f_ref[at, wide_a:])
             store_columns(out_ref, k, q_a, q_b)
             out_ref[k, -16:, :] = codes.T[:16].astype(I32).astype(I16)
 
@@ -394,18 +404,15 @@
     other = lax.ppermute(mine, "mp", core_pairs)
     rows = POLICIES * RANK
     width = wide_a + wide_b + 128
+    scratch = [VMEM((2, 2 * RANK, half), F32), VMEM((2, 2, rows, half), BF16)]
+    total = ((rows, wide_a + wide_b), F32)
+    (own,) = call(own_kernel, [total], [VMEM] * 4, scratch)(owner, mine, acts, cot)
     (pieces,) = call(
         grad_kernel,
         [((4, rows // 4 * (wide_a + wide_b) // 128 + 16, 128), I16)],
         [VMEM] * 5,
-        [
-            VMEM((tokens, 128), F32),
-            VMEM((2, 2 * RANK, tokens), F32),
-            VMEM((2, 2, rows, tokens), BF16),
-            VMEM((rows, wide_a), F32),
-            VMEM((rows, wide_b), F32),
-        ],
-    )(owner, mine, other, acts, cot)
+        scratch + [VMEM(*total)],
+    )(owner, other, acts, cot, own)
     got = lax.all_to_all(pieces, BOTH, 0, 0, tiled=True, axis_index_groups=first)
     (pieces,) = call(
         functools.partial(second_kernel, wide_a, wide_b), [((4, rows // 16, width), I16)], [VMEM]

time: 84.8 us -> 83.9 us (0.989)
  waiting for transfers between devices: 8.54 us -> 7.43 us
    ppermute x1, waiting for transfers between devices: 1.31 us -> 0.1 us  [shards(): other = lax.ppermute(mine, 'mp', core_pairs)]
    pallas_call x0 -> x1, Pallas kernels: none -> 1.2 us  [shards(): call(own_kernel, [total], [VMEM] * 4, scratch)(owner, mine, acts, cot)]
    pallas_call x1, Pallas kernels: 2.68 us -> 1.79 us  [shards(): call(grad_kernel, [((4, rows // 4 * (wide_a + wide_b) // 128 + 16, 128),...]
  transfers between devices with their start and end apart: 4 -> 4, of which waited for: 4 -> 4; matrix products, arithmetic and copies ran while one was open for 0% -> 0% of each run, Pallas kernels for 0% -> 1%
where the time goes in v5:
time: 83.9 us; the launch traced here: 83.6 us
  blocking collectives  39.2 us (47%)
  starting transfers between devices  28.2 us (34%)
  Pallas kernels  7.96 us (9%)
  waiting for transfers between devices  7.43 us (9%)
    all_to_all x1, blocking collectives, shards(): lax.all_to_all(pieces, BOTH, 0, 0, tiled=True, axis_index_groups=first)  18.6 us
    ppermute x1, starting transfers between devices, shards(): far = lax.ppermute(packed, 'mp', far_pairs)  14.8 us
    all_to_all x1, blocking collectives, shards(): lax.all_to_all(pieces, BOTH, 0, 0, tiled=True, axis_index_groups=second)  12 us
    ppermute x1, starting transfers between devices, shards(): lax.ppermute(packed, 'dp', [(i, (i + count // 2) % count) for i in range(...  9.56 us
    all_to_all x1, blocking collectives, shards(): lax.all_to_all(pieces, BOTH, 0, 0, tiled=True, axis_index_groups=third)  8.66 us
    ppermute x1, waiting for transfers between devices, shards(): far = lax.ppermute(packed, 'mp', far_pairs)  4.16 us
    pallas_call x1, Pallas kernels, shards(): call(low_kernel, [((half, 128), F32)] * 2 + [((POLICIES, tokens), I32), (...  3.01 us
    ppermute x1, starting transfers between devices, shards(): got = lax.ppermute(send, 'mp', core_pairs)  1.92 us
  transfers between devices with their start and end apart: 4, of which 4 were waited for; matrix products, arithmetic and copies ran while one was open for 0% of the time, Pallas kernels for 1%

profile of v5, /device:TPU:32, one launch (start us, length us, event | category | flops | bytes accessed | tf_op | source)
XLA Modules:
  0.0 83.6 jit_solution(512388705582753130)
XLA Ops:
  0.6 3.0 %shard_map.104 = (f32[256,128]{1,0:T(8,128)S(1)}, f32[256,128]{1,0:T(8,128)S(1)}, s32[8,512]{1,0:T(8,128)S(1)}, bf16[512,1152]{1,0:T(8,128)(2,1)S(1)}, bf16[512,512]{1,0:T(8,128)(2,1)S(1)}) custom-call(s32[1,8]{1,0:T(1,128)} %lengths_hbm.1, s32[1,8]{1,0:T(1,128)} %policy_hbm.1, f32[1,8]{1,0:T(1,128)} %adv_hbm.1, f32[4,128]{1,0:T(4,128)} %bitcast.2, ...), custom_call_target="tpu_custom_call" | custom-call | tf_op jit(solution)/shard_map/pallas_call | solution.py:384
  3.7 1.9 %collective-permute-start = (f32[256,128]{1,0:T(8,128)S(1)}, f32[256,128]{1,0:T(8,128)S(1)}, u32[]{:S(2)}, u32[]{:S(2)}) collective-permute-start(f32[256,128]{1,0:T(8,128)S(1)} %get-tuple-element.13), channel_id=1, source_target_pairs={{0,1},{1,0},{2,3},{3,2},{4,5},{5,4},{6,7},{7,6},{8,9},{9,8},{10,11... | collective-permute-start | bytes 393224 | tf_op jit(solution)/shard_map/ppermute | solution.py:400
  5.6 1.3 %collective-permute-done.got_ref = f32[256,128]{1,0:T(8,128)S(1)} collective-permute-done((f32[256,128]{1,0:T(8,128)S(1)}, f32[256,128]{1,0:T(8,128)S(1)}, u32[]{:S(2)}, u32[]{:S(2)}) %collective-permute-start) | collective-permute-done | bytes 131104 | tf_op jit(solution)/shard_map/ppermute | solution.py:400
  6.9 0.1 shard_map.105
  7.0 14.8 %collective-permute-start.1 = (s16[272,128]{1,0:T(8,128)(2,1)S(1)}, s16[272,128]{1,0:T(8,128)(2,1)S(1)}, u32[]{:S(2)}, u32[]{:S(2)}) collective-permute-start(s16[272,128]{1,0:T(8,128)(2,1)S(1)} %get-tuple-element.15), channel_id=1, source_target_pairs={{0,2},{2,0},{1,3},{3,1},{4,6},{6,4},{5,7},{7,5},{8,10},{10,8},{9,1... | collective-permute-start | bytes 208904 | tf_op jit(solution)/shard_map/ppermute | solution.py:402
  21.8 4.2 %collective-permute-done.1.got_ref = s16[272,128]{1,0:T(8,128)(2,1)S(1)} collective-permute-done((s16[272,128]{1,0:T(8,128)(2,1)S(1)}, s16[272,128]{1,0:T(8,128)(2,1)S(1)}, u32[]{:S(2)}, u32[]{:S(2)}) %collective-permute-start.1) | collective-permute-done | bytes 69664 | tf_op jit(solution)/shard_map/ppermute | solution.py:402
  26.0 1.9 %collective-permute-start.2 = (f32[256,128]{1,0:T(8,128)S(1)}, f32[256,128]{1,0:T(8,128)S(1)}, u32[]{:S(2)}, u32[]{:S(2)}) collective-permute-start(f32[256,128]{1,0:T(8,128)S(1)} %shard_map.106.half_ref), channel_id=1, source_target_pairs={{0,1},{1,0},{2,3},{3,2},{4,5},{5,4},{6,7},{7,6},{8,9},{9,8},{10,11... | collective-permute-start | bytes 393224 | tf_op jit(solution)/shard_map/ppermute | solution.py:404
  27.9 1.2 %shard_map.107.sum_ref = f32[512,1664]{1,0:T(8,128)S(1)} custom-call(s32[8,512]{1,0:T(8,128)S(1)} %get-tuple-element.11.owner_ref, f32[256,128]{1,0:T(8,128)S(1)} %shard_map.106.half_ref, bf16[512,1152]{1,0:T(8,128)(2,1)S(1)} %get-tuple-element.16.acts_ref, bf16[512,512]{1,0:T(8,128)(2,1)S(1)} %get-tuple-element.17.cot_ref), custom_call_target="tpu_custom_call" | custom-call | tf_op jit(solution)/shard_map/pallas_call | solution.py:409
  29.1 0.1 collective-permute-done.2.half_ref
  29.2 1.8 %shard_map.108 = s16[4,1680,128]{2,1,0:T(8,128)(2,1)S(1)} custom-call(s32[8,512]{1,0:T(8,128)S(1)} %get-tuple-element.11.owner_ref, f32[256,128]{1,0:T(8,128)S(1)} %collective-permute-done.2.half_ref, bf16[512,1152]{1,0:T(8,128)(2,1)S(1)} %get-tuple-element.16.acts_ref, bf16[512,512]{1,0:T(8,128)(2,1)S(1)} %get-tuple-element.17.cot_ref, ...), custom_call_target="tpu_custom_call" | custom-call | tf_op jit(solution)/shard_map/pallas_call | solution.py:410
  31.0 18.6 %all_to_all.15.got_ref = s16[4,1680,128]{2,1,0:T(8,128)(2,1)S(1)} all-to-all(s16[4,1680,128]{2,1,0:T(8,128)(2,1)S(1)} %shard_map.108), channel_id=1, replica_groups={{0,16,32,48},{1,5,9,13},{4,20,36,52},{17,21,25,29},{8,24,40,56},{33,37,..., dimensions={0} | all-to-all | bytes 3440640 | tf_op jit(solution)/shard_map/all_to_all | solution.py:416
  49.6 0.8 shard_map.109
  50.4 12.0 %all_to_all.16.got_ref = s16[4,32,1792]{2,1,0:T(8,128)(2,1)S(1)} all-to-all(s16[4,32,1792]{2,1,0:T(8,128)(2,1)S(1)} %shard_map.109), channel_id=1, replica_groups={{0,4,8,12},{1,17,33,49},{16,20,24,28},{5,21,37,53},{32,36,40,44},{9,25,..., dimensions={0} | all-to-all | bytes 917504 | tf_op jit(solution)/shard_map/all_to_all | solution.py:420
  62.4 0.3 shard_map.110
  62.7 8.7 %all_to_all.17.got_ref = s16[4,112,128]{2,1,0:T(8,128)(2,1)S(1)} all-to-all(s16[4,112,128]{2,1,0:T(8,128)(2,1)S(1)} %shard_map.110), channel_id=1, replica_groups={{0,64,128,192},{1,65,129,193},{2,66,130,194},{3,67,131,195},{4,68,132,1..., dimensions={0} | all-to-all | bytes 229376 | tf_op jit(solution)/shard_map/all_to_all | solution.py:425
  71.4 0.1 shard_map.111
  71.5 9.6 %collective-permute-start.3 = (s16[64,128]{1,0:T(8,128)(2,1)S(1)}, s16[64,128]{1,0:T(8,128)(2,1)S(1)}, u32[]{:S(2)}, u32[]{:S(2)}) collective-permute-start(s16[64,128]{1,0:T(8,128)(2,1)S(1)} %get-tuple-element.19), channel_id=1, source_target_pairs={{0,256},{4,260},{8,264},{12,268},{16,272},{20,276},{24,280},{28,28... | collective-permute-start | bytes 49160 | tf_op jit(solution)/shard_map/ppermute | solution.py:432
  81.1 1.9 %collective-permute-done.3.got_ref = s16[64,128]{1,0:T(8,128)(2,1)S(1)} collective-permute-done((s16[64,128]{1,0:T(8,128)(2,1)S(1)}, s16[64,128]{1,0:T(8,128)(2,1)S(1)}, u32[]{:S(2)}, u32[]{:S(2)}) %collective-permute-start.3) | collective-permute-done | bytes 16416 | tf_op jit(solution)/shard_map/ppermute | solution.py:432
  82.9 0.6 shard_map.112
  (1 shorter events, 0.0 us)
Async XLA Ops:
  3.7 3.2 %collective-permute-start = (f32[256,128]{1,0:T(8,128)S(1)}, f32[256,128]{1,0:T(8,128)S(1)}, u32[]{:S(2)}, u32[]{:S(2)}) collective-permute-start(f32[256,128]{1,0:T(8,128)S(1)} %get-tuple-element.13), channel_id=1, source_target_pairs={{0,1},{1,0},{2,3},{3,2},{4,5},{5,4},{6,7},{7,6},{8,9},{9,8},{10,11... | collective-permute-start | bytes 393224 | tf_op jit(solution)/shard_map/ppermute | solution.py:400
  7.0 19.0 %collective-permute-start.1 = (s16[272,128]{1,0:T(8,128)(2,1)S(1)}, s16[272,128]{1,0:T(8,128)(2,1)S(1)}, u32[]{:S(2)}, u32[]{:S(2)}) collective-permute-start(s16[272,128]{1,0:T(8,128)(2,1)S(1)} %get-tuple-element.15), channel_id=1, source_target_pairs={{0,2},{2,0},{1,3},{3,1},{4,6},{6,4},{5,7},{7,5},{8,10},{10,8},{9,1... | collective-permute-start | bytes 208904 | tf_op jit(solution)/shard_map/ppermute | solution.py:402
  26.0 3.2 %collective-permute-start.2 = (f32[256,128]{1,0:T(8,128)S(1)}, f32[256,128]{1,0:T(8,128)S(1)}, u32[]{:S(2)}, u32[]{:S(2)}) collective-permute-start(f32[256,128]{1,0:T(8,128)S(1)} %shard_map.106.half_ref), channel_id=1, source_target_pairs={{0,1},{1,0},{2,3},{3,2},{4,5},{5,4},{6,7},{7,6},{8,9},{9,8},{10,11... | collective-permute-start | bytes 393224 | tf_op jit(solution)/shard_map/ppermute | solution.py:404
  71.5 11.4 %collective-permute-start.3 = (s16[64,128]{1,0:T(8,128)(2,1)S(1)}, s16[64,128]{1,0:T(8,128)(2,1)S(1)}, u32[]{:S(2)}, u32[]{:S(2)}) collective-permute-start(s16[64,128]{1,0:T(8,128)(2,1)S(1)} %get-tuple-element.19), channel_id=1, source_target_pairs={{0,256},{4,260},{8,264},{12,268},{16,272},{20,276},{24,280},{28,28... | collective-permute-start | bytes 49160 | tf_op jit(solution)/shard_map/ppermute | solution.py:432

commit v6 on v5

--- a/solution.py
+++ b/solution.py
@@ -49,11 +49,10 @@
 
 def low_kernel(
     lengths_hbm, policy_hbm, adv_hbm, old_hbm, new_hbm, acts_hbm, cot_hbm, down_hbm, up_hbm,
-    keep_ref, send_ref, owner_ref, acts_ref, cot_ref,
-    x_ref, lengths_ref, policy_ref, adv_ref, old_ref, new_ref, down_ref, up_ref, sems,
+    send_ref, owner_ref, acts_ref, cot_ref, down_ref, up_ref, member_ref, weight_ref,
+    lengths_ref, policy_ref, adv_ref, old_ref, new_ref, sems,
 ):
     tokens, wide_a = acts_ref.shape
-    half = tokens // 2
     pairs = [
         (lengths_hbm, lengths_ref),
         (policy_hbm, policy_ref),
@@ -91,30 +90,43 @@
     groups = ratio.shape[0]
     ratio = jnp.concatenate([ratio, jnp.zeros((128 - groups, 128), F32)], axis=0).T
     ratio = jnp.concatenate([ratio[:, j : j + 1] for j in range(groups)], axis=0)
-    weight = factor * ratio
+    weight_ref[...] = factor * ratio
+    member_ref[...] = owner
+
+    def wait(group):
+        for copy in copies[group]:
+            copy.wait()
+
+    half_products(True, acts_ref, cot_ref, down_ref, up_ref, member_ref, weight_ref, send_ref, wait)
+
+
+def half_products(other, acts_ref, cot_ref, down_ref, up_ref, member_ref, weight_ref, out_ref, wait):
+    half = out_ref.shape[0]
+    core = lax.rem(lax.axis_index("mp"), 2)
+    tokens = pl.ds(pl.multiple_of((1 - core if other else core) * half, half), half)
+    owner = member_ref[tokens, :]
+    lane = lax.broadcasted_iota(I32, (half, 128), 1)
 
     def own(full):
-        total = jnp.zeros((tokens, 128), F32)
+        total = jnp.zeros((half, 128), F32)
         for j in range(POLICIES // 2):
             mine = owner == 2 * j + jnp.where(lane >= RANK, 1, 0)
             total = total + jnp.where(mine, full[:, j * 128 : (j + 1) * 128], 0.0)
         return total + pltpu.roll(total, RANK, 1)
 
-    copies[5].wait()
-    copies[6].wait()
+    wait(slice(5, 7))
     low_out = own(
-        lax.dot_general(cot_ref[...], up_ref[...], (((1,), (1,)), ((), ())), preferred_element_type=F32)
+        lax.dot_general(cot_ref[tokens, :], up_ref[...], (((1,), (1,)), ((), ())), preferred_element_type=F32)
     )
-    copies[7].wait()
-    copies[8].wait()
-    low_in = jnp.dot(acts_ref[:, :CUT], down_ref[:CUT, :], preferred_element_type=F32)
-    copies[9].wait()
-    copies[10].wait()
-    low_in = own(low_in + jnp.dot(acts_ref[:, CUT:], down_ref[CUT:, :], preferred_element_type=F32))
-    x_ref[...] = jnp.where(lane < RANK, low_in, low_out) * weight
-    core = lax.rem(lax.axis_index("mp"), 2)
-    keep_ref[...] = x_ref[pl.ds(pl.multiple_of(core * half, half), half), :]
-    send_ref[...] = x_ref[pl.ds(pl.multiple_of((1 - core) * half, half), half), :]
+    wait(slice(7, 9))
+    low_in = jnp.dot(acts_ref[tokens, :CUT], down_ref[:CUT, :], preferred_element_type=F32)
+    wait(slice(9, 11))
+    low_in = own(low_in + jnp.dot(acts_ref[tokens, CUT:], down_ref[CUT:, :], preferred_element_type=F32))
+    out_ref[...] = jnp.where(lane < RANK, low_in, low_out) * weight_ref[tokens, :]
+
+
+def keep_kernel(acts_ref, cot_ref, down_ref, up_ref, member_ref, weight_ref, out_ref):
+    half_products(False, acts_ref, cot_ref, down_ref, up_ref, member_ref, weight_ref, out_ref, lambda group: None)
 
 
 BLOCKS = 4
@@ -381,23 +393,30 @@
     core_pairs = [(0, 1), (1, 0), (2, 3), (3, 2)]
     far_pairs = [(0, 2), (2, 0), (1, 3), (3, 1)]
     lines = (tokens // 128, 128)
-    keep, send, owner, acts, cot = call(
+    send, owner, acts, cot, down, up, member, weight = call(
         low_kernel,
-        [((half, 128), F32)] * 2 + [((POLICIES, tokens), I32), (acts.shape, BF16), (cot.shape, BF16)],
+        [
+            ((half, 128), F32),
+            ((POLICIES, tokens), I32),
+            (acts.shape, BF16),
+            (cot.shape, BF16),
+            (down.shape, BF16),
+            (up.shape, BF16),
+            ((tokens, 128), I32),
+            ((tokens, 128), F32),
+        ],
         [HBM] * 9,
         [
-            VMEM((tokens, 128), F32),
             SMEM(lengths.shape, I32),
             SMEM(policy.shape, I32),
             SMEM(advantages.shape, F32),
             VMEM(lines, F32),
             VMEM(lines, F32),
-            VMEM(down.shape, BF16),
-            VMEM(up.shape, BF16),
             pltpu.SemaphoreType.DMA((11,)),
         ],
     )(*map(in_hbm, (lengths, policy, advantages, old.reshape(lines), new.reshape(lines), acts, cot, down, up)))
     got = lax.ppermute(send, "mp", core_pairs)
+    (keep,) = call(keep_kernel, [((half, 128), F32)], [VMEM] * 6)(acts, cot, down, up, member, weight)
     part, packed = call(pack_kernel, [((half, 128), F32), ((half + 16, 128), I16)], [VMEM] * 2)(keep, got)
     far = lax.ppermute(packed, "mp", far_pairs)
     (mine,) = call(unpack_kernel, [((half, 128), F32)], [VMEM] * 2)(part, far)

time: 83.9 us -> 83.4 us (level)
    pallas_call x1 -> x2, Pallas kernels: 3.01 us -> 3.39 us  [the longest x1 2.63 us: shards(): call(low_kernel, [((half, 128), F32), ((POLICIES, tokens), I32), (acts.sh...]
  transfers between devices with their start and end apart: 4 -> 4, of which waited for: 4 -> 4; matrix products, arithmetic and copies ran while one was open for 0% -> 0% of each run, Pallas kernels for 1% -> 2%
where the time goes in v6:
time: 83.4 us; the launch traced here: 83.1 us
  blocking collectives  39.2 us (47%)
  starting transfers between devices  28.2 us (34%)
  Pallas kernels  8.34 us (10%)
  waiting for transfers between devices  6.64 us (8%)
    all_to_all x1, blocking collectives, shards(): lax.all_to_all(pieces, BOTH, 0, 0, tiled=True, axis_index_groups=first)  18.6 us
    ppermute x1, starting transfers between devices, shards(): far = lax.ppermute(packed, 'mp', far_pairs)  14.8 us
    all_to_all x1, blocking collectives, shards(): lax.all_to_all(pieces, BOTH, 0, 0, tiled=True, axis_index_groups=second)  12 us
    ppermute x1, starting transfers between devices, shards(): lax.ppermute(packed, 'dp', [(i, (i + count // 2) % count) for i in range(...  9.5 us
    all_to_all x1, blocking collectives, shards(): lax.all_to_all(pieces, BOTH, 0, 0, tiled=True, axis_index_groups=third)  8.64 us
    ppermute x1, waiting for transfers between devices, shards(): far = lax.ppermute(packed, 'mp', far_pairs)  4.16 us
    pallas_call x1, Pallas kernels, shards(): call(low_kernel, [((half, 128), F32), ((POLICIES, tokens), I32), (acts.sh...  2.63 us
    ppermute x1, starting transfers between devices, shards(): got = lax.ppermute(send, 'mp', core_pairs)  1.92 us
  transfers between devices with their start and end apart: 4, of which 4 were waited for; matrix products, arithmetic and copies ran while one was open for 0% of the time, Pallas kernels for 2%

profile of v6, /device:TPU:32, one launch (start us, length us, event | category | flops | bytes accessed | tf_op | source)
XLA Modules:
  0.0 83.1 jit_solution(10039253216771963027)
XLA Ops:
  0.6 2.6 %shard_map.104 = (f32[256,128]{1,0:T(8,128)S(1)}, s32[8,512]{1,0:T(8,128)S(1)}, bf16[512,1152]{1,0:T(8,128)(2,1)S(1)}, bf16[512,512]{1,0:T(8,128)(2,1)S(1)}, bf1...) custom-call(s32[1,8]{1,0:T(1,128)} %lengths_hbm.1, ...), custom_call_target="tpu_custom_call" | custom-call | tf_op jit(solution)/shard_map/pallas_call | solution.py:396
  3.3 1.9 %collective-permute-start = (f32[256,128]{1,0:T(8,128)S(1)}, f32[256,128]{1,0:T(8,128)S(1)}, u32[]{:S(2)}, u32[]{:S(2)}) collective-permute-start(f32[256,128]{1,0:T(8,128)S(1)} %get-tuple-element.21), channel_id=1, source_target_pairs={{0,1},{1,0},{2,3},{3,2},{4,5},{5,4},{6,7},{7,6},{8,9},{9,8},{10,11... | collective-permute-start | bytes 393224 | tf_op jit(solution)/shard_map/ppermute | solution.py:418
  5.2 0.8 shard_map.105.keep_ref
  6.0 0.5 collective-permute-done.got_ref
  6.5 0.1 shard_map.106
  6.6 14.8 %collective-permute-start.1 = (s16[272,128]{1,0:T(8,128)(2,1)S(1)}, s16[272,128]{1,0:T(8,128)(2,1)S(1)}, u32[]{:S(2)}, u32[]{:S(2)}) collective-permute-start(s16[272,128]{1,0:T(8,128)(2,1)S(1)} %get-tuple-element.23), channel_id=1, source_target_pairs={{0,2},{2,0},{1,3},{3,1},{4,6},{6,4},{5,7},{7,5},{8,10},{10,8},{9,1... | collective-permute-start | bytes 208904 | tf_op jit(solution)/shard_map/ppermute | solution.py:421
  21.4 4.2 %collective-permute-done.1.got_ref = s16[272,128]{1,0:T(8,128)(2,1)S(1)} collective-permute-done((s16[272,128]{1,0:T(8,128)(2,1)S(1)}, s16[272,128]{1,0:T(8,128)(2,1)S(1)}, u32[]{:S(2)}, u32[]{:S(2)}) %collective-permute-start.1) | collective-permute-done | bytes 69664 | tf_op jit(solution)/shard_map/ppermute | solution.py:421
  25.6 1.9 %collective-permute-start.2 = (f32[256,128]{1,0:T(8,128)S(1)}, f32[256,128]{1,0:T(8,128)S(1)}, u32[]{:S(2)}, u32[]{:S(2)}) collective-permute-start(f32[256,128]{1,0:T(8,128)S(1)} %shard_map.107.half_ref), channel_id=1, source_target_pairs={{0,1},{1,0},{2,3},{3,2},{4,5},{5,4},{6,7},{7,6},{8,9},{9,8},{10,11... | collective-permute-start | bytes 393224 | tf_op jit(solution)/shard_map/ppermute | solution.py:423
  27.5 1.2 %shard_map.108.sum_ref = f32[512,1664]{1,0:T(8,128)S(1)} custom-call(s32[8,512]{1,0:T(8,128)S(1)} %get-tuple-element.14.owner_ref, f32[256,128]{1,0:T(8,128)S(1)} %shard_map.107.half_ref, bf16[512,1152]{1,0:T(8,128)(2,1)S(1)} %get-tuple-element.15.acts_ref, bf16[512,512]{1,0:T(8,128)(2,1)S(1)} %get-tuple-element.16.cot_ref), custom_call_target="tpu_custom_call" | custom-call | tf_op jit(solution)/shard_map/pallas_call | solution.py:428
  28.7 0.1 collective-permute-done.2.half_ref
  28.8 1.8 %shard_map.109 = s16[4,1680,128]{2,1,0:T(8,128)(2,1)S(1)} custom-call(s32[8,512]{1,0:T(8,128)S(1)} %get-tuple-element.14.owner_ref, f32[256,128]{1,0:T(8,128)S(1)} %collective-permute-done.2.half_ref, bf16[512,1152]{1,0:T(8,128)(2,1)S(1)} %get-tuple-element.15.acts_ref, bf16[512,512]{1,0:T(8,128)(2,1)S(1)} %get-tuple-element.16.cot_ref, ...), custom_call_target="tpu_custom_call" | custom-call | tf_op jit(solution)/shard_map/pallas_call | solution.py:429
  30.6 18.6 %all_to_all.15.got_ref = s16[4,1680,128]{2,1,0:T(8,128)(2,1)S(1)} all-to-all(s16[4,1680,128]{2,1,0:T(8,128)(2,1)S(1)} %shard_map.109), channel_id=1, replica_groups={{0,16,32,48},{1,5,9,13},{4,20,36,52},{17,21,25,29},{8,24,40,56},{33,37,..., dimensions={0} | all-to-all | bytes 3440640 | tf_op jit(solution)/shard_map/all_to_all | solution.py:435
  49.2 0.8 shard_map.110
  50.0 12.0 %all_to_all.16.got_ref = s16[4,32,1792]{2,1,0:T(8,128)(2,1)S(1)} all-to-all(s16[4,32,1792]{2,1,0:T(8,128)(2,1)S(1)} %shard_map.110), channel_id=1, replica_groups={{0,4,8,12},{1,17,33,49},{16,20,24,28},{5,21,37,53},{32,36,40,44},{9,25,..., dimensions={0} | all-to-all | bytes 917504 | tf_op jit(solution)/shard_map/all_to_all | solution.py:439
  62.0 0.3 shard_map.111
  62.3 8.6 %all_to_all.17.got_ref = s16[4,112,128]{2,1,0:T(8,128)(2,1)S(1)} all-to-all(s16[4,112,128]{2,1,0:T(8,128)(2,1)S(1)} %shard_map.111), channel_id=1, replica_groups={{0,64,128,192},{1,65,129,193},{2,66,130,194},{3,67,131,195},{4,68,132,1..., dimensions={0} | all-to-all | bytes 229376 | tf_op jit(solution)/shard_map/all_to_all | solution.py:444
  71.0 0.1 shard_map.112
  71.1 9.5 %collective-permute-start.3 = (s16[64,128]{1,0:T(8,128)(2,1)S(1)}, s16[64,128]{1,0:T(8,128)(2,1)S(1)}, u32[]{:S(2)}, u32[]{:S(2)}) collective-permute-start(s16[64,128]{1,0:T(8,128)(2,1)S(1)} %get-tuple-element.25), channel_id=1, source_target_pairs={{0,256},{4,260},{8,264},{12,268},{16,272},{20,276},{24,280},{28,28... | collective-permute-start | bytes 49160 | tf_op jit(solution)/shard_map/ppermute | solution.py:451
  80.6 1.8 %collective-permute-done.3.got_ref = s16[64,128]{1,0:T(8,128)(2,1)S(1)} collective-permute-done((s16[64,128]{1,0:T(8,128)(2,1)S(1)}, s16[64,128]{1,0:T(8,128)(2,1)S(1)}, u32[]{:S(2)}, u32[]{:S(2)}) %collective-permute-start.3) | collective-permute-done | bytes 16416 | tf_op jit(solution)/shard_map/ppermute | solution.py:451
  82.5 0.6 shard_map.113
  (1 shorter events, 0.0 us)
Async XLA Ops:
  3.3 3.2 %collective-permute-start = (f32[256,128]{1,0:T(8,128)S(1)}, f32[256,128]{1,0:T(8,128)S(1)}, u32[]{:S(2)}, u32[]{:S(2)}) collective-permute-start(f32[256,128]{1,0:T(8,128)S(1)} %get-tuple-element.21), channel_id=1, source_target_pairs={{0,1},{1,0},{2,3},{3,2},{4,5},{5,4},{6,7},{7,6},{8,9},{9,8},{10,11... | collective-permute-start | bytes 393224 | tf_op jit(solution)/shard_map/ppermute | solution.py:418
  6.6 19.0 %collective-permute-start.1 = (s16[272,128]{1,0:T(8,128)(2,1)S(1)}, s16[272,128]{1,0:T(8,128)(2,1)S(1)}, u32[]{:S(2)}, u32[]{:S(2)}) collective-permute-start(s16[272,128]{1,0:T(8,128)(2,1)S(1)} %get-tuple-element.23), channel_id=1, source_target_pairs={{0,2},{2,0},{1,3},{3,1},{4,6},{6,4},{5,7},{7,5},{8,10},{10,8},{9,1... | collective-permute-start | bytes 208904 | tf_op jit(solution)/shard_map/ppermute | solution.py:421
  25.6 3.2 %collective-permute-start.2 = (f32[256,128]{1,0:T(8,128)S(1)}, f32[256,128]{1,0:T(8,128)S(1)}, u32[]{:S(2)}, u32[]{:S(2)}) collective-permute-start(f32[256,128]{1,0:T(8,128)S(1)} %shard_map.107.half_ref), channel_id=1, source_target_pairs={{0,1},{1,0},{2,3},{3,2},{4,5},{5,4},{6,7},{7,6},{8,9},{9,8},{10,11... | collective-permute-start | bytes 393224 | tf_op jit(solution)/shard_map/ppermute | solution.py:423
  71.1 11.3 %collective-permute-start.3 = (s16[64,128]{1,0:T(8,128)(2,1)S(1)}, s16[64,128]{1,0:T(8,128)(2,1)S(1)}, u32[]{:S(2)}, u32[]{:S(2)}) collective-permute-start(s16[64,128]{1,0:T(8,128)(2,1)S(1)} %get-tuple-element.25), channel_id=1, source_target_pairs={{0,256},{4,260},{8,264},{12,268},{16,272},{20,276},{24,280},{28,28... | collective-permute-start | bytes 49160 | tf_op jit(solution)/shard_map/ppermute | solution.py:451

commit v7 on v6

--- a/solution.py
+++ b/solution.py
@@ -53,18 +53,24 @@
     lengths_ref, policy_ref, adv_ref, old_ref, new_ref, sems,
 ):
     tokens, wide_a = acts_ref.shape
+    half = tokens // 2
+    core = lax.rem(lax.axis_index("mp"), 2)
+    sent = pl.ds(pl.multiple_of((1 - core) * half, half), half)
+    kept = pl.ds(pl.multiple_of(core * half, half), half)
     pairs = [
         (lengths_hbm, lengths_ref),
         (policy_hbm, policy_ref),
         (adv_hbm, adv_ref),
         (old_hbm, old_ref),
         (new_hbm, new_ref),
-        (cot_hbm, cot_ref),
+        (cot_hbm.at[sent, :], cot_ref.at[sent, :]),
         (up_hbm, up_ref),
-        (acts_hbm.at[:, :CUT], acts_ref.at[:, :CUT]),
+        (acts_hbm.at[sent, :CUT], acts_ref.at[sent, :CUT]),
         (down_hbm.at[:CUT, :], down_ref.at[:CUT, :]),
-        (acts_hbm.at[:, CUT:], acts_ref.at[:, CUT:]),
+        (acts_hbm.at[sent, CUT:], acts_ref.at[sent, CUT:]),
         (down_hbm.at[CUT:, :], down_ref.at[CUT:, :]),
+        (cot_hbm.at[kept, :], cot_ref.at[kept, :]),
+        (acts_hbm.at[kept, :], acts_ref.at[kept, :]),
     ]
     copies = [pltpu.make_async_copy(src, dst, sems.at[i]) for i, (src, dst) in enumerate(pairs)]
     for copy in copies:
@@ -98,6 +104,7 @@
             copy.wait()
 
     half_products(True, acts_ref, cot_ref, down_ref, up_ref, member_ref, weight_ref, send_ref, wait)
+    wait(slice(11, 13))
 
 
 def half_products(other, acts_ref, cot_ref, down_ref, up_ref, member_ref, weight_ref, out_ref, wait):
@@ -412,7 +419,7 @@
             SMEM(advantages.shape, F32),
             VMEM(lines, F32),
             VMEM(lines, F32),
-            pltpu.SemaphoreType.DMA((11,)),
+            pltpu.SemaphoreType.DMA((13,)),
         ],
     )(*map(in_hbm, (lengths, policy, advantages, old.reshape(lines), new.reshape(lines), acts, cot, down, up)))
     got = lax.ppermute(send, "mp", core_pairs)

time: 83.4 us -> 83.3 us (level)
  no operation moved by 1% of the time
where the time goes in v7:
time: 83.3 us; the launch traced here: 83 us
  blocking collectives  39.2 us (47%)
  starting transfers between devices  28.3 us (34%)
  Pallas kernels  8.1 us (10%)
  waiting for transfers between devices  6.63 us (8%)
    all_to_all x1, blocking collectives, shards(): lax.all_to_all(pieces, BOTH, 0, 0, tiled=True, axis_index_groups=first)  18.6 us
    ppermute x1, starting transfers between devices, shards(): far = lax.ppermute(packed, 'mp', far_pairs)  14.8 us
    all_to_all x1, blocking collectives, shards(): lax.all_to_all(pieces, BOTH, 0, 0, tiled=True, axis_index_groups=second)  12 us
    ppermute x1, starting transfers between devices, shards(): lax.ppermute(packed, 'dp', [(i, (i + count // 2) % count) for i in range(...  9.61 us
    all_to_all x1, blocking collectives, shards(): lax.all_to_all(pieces, BOTH, 0, 0, tiled=True, axis_index_groups=third)  8.65 us
    ppermute x1, waiting for transfers between devices, shards(): far = lax.ppermute(packed, 'mp', far_pairs)  4.16 us
    pallas_call x1, Pallas kernels, shards(): call(low_kernel, [((half, 128), F32), ((POLICIES, tokens), I32), (acts.sh...  2.4 us
    ppermute x1, starting transfers between devices, shards(): got = lax.ppermute(send, 'mp', core_pairs)  1.92 us
  transfers between devices with their start and end apart: 4, of which 4 were waited for; matrix products, arithmetic and copies ran while one was open for 0% of the time, Pallas kernels for 2%

profile of v7, /device:TPU:32, one launch (start us, length us, event | category | flops | bytes accessed | tf_op | source)
XLA Modules:
  0.0 83.0 jit_solution(7447873989022128092)
XLA Ops:
  0.6 2.4 %shard_map.104 = (f32[256,128]{1,0:T(8,128)S(1)}, s32[8,512]{1,0:T(8,128)S(1)}, bf16[512,1152]{1,0:T(8,128)(2,1)S(1)}, bf16[512,512]{1,0:T(8,128)(2,1)S(1)}, bf1...) custom-call(s32[1,8]{1,0:T(1,128)} %lengths_hbm.1, ...), custom_call_target="tpu_custom_call" | custom-call | tf_op jit(solution)/shard_map/pallas_call | solution.py:403
  3.0 1.9 %collective-permute-start = (f32[256,128]{1,0:T(8,128)S(1)}, f32[256,128]{1,0:T(8,128)S(1)}, u32[]{:S(2)}, u32[]{:S(2)}) collective-permute-start(f32[256,128]{1,0:T(8,128)S(1)} %get-tuple-element.21), channel_id=1, source_target_pairs={{0,1},{1,0},{2,3},{3,2},{4,5},{5,4},{6,7},{7,6},{8,9},{9,8},{10,11... | collective-permute-start | bytes 393224 | tf_op jit(solution)/shard_map/ppermute | solution.py:425
  5.0 0.8 shard_map.105.keep_ref
  5.7 0.5 collective-permute-done.got_ref
  6.3 0.1 shard_map.106
  6.3 14.8 %collective-permute-start.1 = (s16[272,128]{1,0:T(8,128)(2,1)S(1)}, s16[272,128]{1,0:T(8,128)(2,1)S(1)}, u32[]{:S(2)}, u32[]{:S(2)}) collective-permute-start(s16[272,128]{1,0:T(8,128)(2,1)S(1)} %get-tuple-element.23), channel_id=1, source_target_pairs={{0,2},{2,0},{1,3},{3,1},{4,6},{6,4},{5,7},{7,5},{8,10},{10,8},{9,1... | collective-permute-start | bytes 208904 | tf_op jit(solution)/shard_map/ppermute | solution.py:428
  21.2 4.2 %collective-permute-done.1.got_ref = s16[272,128]{1,0:T(8,128)(2,1)S(1)} collective-permute-done((s16[272,128]{1,0:T(8,128)(2,1)S(1)}, s16[272,128]{1,0:T(8,128)(2,1)S(1)}, u32[]{:S(2)}, u32[]{:S(2)}) %collective-permute-start.1) | collective-permute-done | bytes 69664 | tf_op jit(solution)/shard_map/ppermute | solution.py:428
  25.4 1.9 %collective-permute-start.2 = (f32[256,128]{1,0:T(8,128)S(1)}, f32[256,128]{1,0:T(8,128)S(1)}, u32[]{:S(2)}, u32[]{:S(2)}) collective-permute-start(f32[256,128]{1,0:T(8,128)S(1)} %shard_map.107.half_ref), channel_id=1, source_target_pairs={{0,1},{1,0},{2,3},{3,2},{4,5},{5,4},{6,7},{7,6},{8,9},{9,8},{10,11... | collective-permute-start | bytes 393224 | tf_op jit(solution)/shard_map/ppermute | solution.py:430
  27.3 1.2 %shard_map.108.sum_ref = f32[512,1664]{1,0:T(8,128)S(1)} custom-call(s32[8,512]{1,0:T(8,128)S(1)} %get-tuple-element.14.owner_ref, f32[256,128]{1,0:T(8,128)S(1)} %shard_map.107.half_ref, bf16[512,1152]{1,0:T(8,128)(2,1)S(1)} %get-tuple-element.15.acts_ref, bf16[512,512]{1,0:T(8,128)(2,1)S(1)} %get-tuple-element.16.cot_ref), custom_call_target="tpu_custom_call" | custom-call | tf_op jit(solution)/shard_map/pallas_call | solution.py:435
  28.5 0.1 collective-permute-done.2.half_ref
  28.6 1.8 %shard_map.109 = s16[4,1680,128]{2,1,0:T(8,128)(2,1)S(1)} custom-call(s32[8,512]{1,0:T(8,128)S(1)} %get-tuple-element.14.owner_ref, f32[256,128]{1,0:T(8,128)S(1)} %collective-permute-done.2.half_ref, bf16[512,1152]{1,0:T(8,128)(2,1)S(1)} %get-tuple-element.15.acts_ref, bf16[512,512]{1,0:T(8,128)(2,1)S(1)} %get-tuple-element.16.cot_ref, ...), custom_call_target="tpu_custom_call" | custom-call | tf_op jit(solution)/shard_map/pallas_call | solution.py:436
  30.4 18.6 %all_to_all.15.got_ref = s16[4,1680,128]{2,1,0:T(8,128)(2,1)S(1)} all-to-all(s16[4,1680,128]{2,1,0:T(8,128)(2,1)S(1)} %shard_map.109), channel_id=1, replica_groups={{0,16,32,48},{1,5,9,13},{4,20,36,52},{17,21,25,29},{8,24,40,56},{33,37,..., dimensions={0} | all-to-all | bytes 3440640 | tf_op jit(solution)/shard_map/all_to_all | solution.py:442
  49.0 0.8 shard_map.110
  49.8 12.0 %all_to_all.16.got_ref = s16[4,32,1792]{2,1,0:T(8,128)(2,1)S(1)} all-to-all(s16[4,32,1792]{2,1,0:T(8,128)(2,1)S(1)} %shard_map.110), channel_id=1, replica_groups={{0,4,8,12},{1,17,33,49},{16,20,24,28},{5,21,37,53},{32,36,40,44},{9,25,..., dimensions={0} | all-to-all | bytes 917504 | tf_op jit(solution)/shard_map/all_to_all | solution.py:446
  61.8 0.3 shard_map.111
  62.1 8.6 %all_to_all.17.got_ref = s16[4,112,128]{2,1,0:T(8,128)(2,1)S(1)} all-to-all(s16[4,112,128]{2,1,0:T(8,128)(2,1)S(1)} %shard_map.111), channel_id=1, replica_groups={{0,64,128,192},{1,65,129,193},{2,66,130,194},{3,67,131,195},{4,68,132,1..., dimensions={0} | all-to-all | bytes 229376 | tf_op jit(solution)/shard_map/all_to_all | solution.py:451
  70.7 0.1 shard_map.112
  70.9 9.6 %collective-permute-start.3 = (s16[64,128]{1,0:T(8,128)(2,1)S(1)}, s16[64,128]{1,0:T(8,128)(2,1)S(1)}, u32[]{:S(2)}, u32[]{:S(2)}) collective-permute-start(s16[64,128]{1,0:T(8,128)(2,1)S(1)} %get-tuple-element.25), channel_id=1, source_target_pairs={{0,256},{4,260},{8,264},{12,268},{16,272},{20,276},{24,280},{28,28... | collective-permute-start | bytes 49160 | tf_op jit(solution)/shard_map/ppermute | solution.py:458
  80.5 1.8 %collective-permute-done.3.got_ref = s16[64,128]{1,0:T(8,128)(2,1)S(1)} collective-permute-done((s16[64,128]{1,0:T(8,128)(2,1)S(1)}, s16[64,128]{1,0:T(8,128)(2,1)S(1)}, u32[]{:S(2)}, u32[]{:S(2)}) %collective-permute-start.3) | collective-permute-done | bytes 16416 | tf_op jit(solution)/shard_map/ppermute | solution.py:458
  82.3 0.6 shard_map.113
  (1 shorter events, 0.0 us)
Async XLA Ops:
  3.0 3.2 %collective-permute-start = (f32[256,128]{1,0:T(8,128)S(1)}, f32[256,128]{1,0:T(8,128)S(1)}, u32[]{:S(2)}, u32[]{:S(2)}) collective-permute-start(f32[256,128]{1,0:T(8,128)S(1)} %get-tuple-element.21), channel_id=1, source_target_pairs={{0,1},{1,0},{2,3},{3,2},{4,5},{5,4},{6,7},{7,6},{8,9},{9,8},{10,11... | collective-permute-start | bytes 393224 | tf_op jit(solution)/shard_map/ppermute | solution.py:425
  6.3 19.0 %collective-permute-start.1 = (s16[272,128]{1,0:T(8,128)(2,1)S(1)}, s16[272,128]{1,0:T(8,128)(2,1)S(1)}, u32[]{:S(2)}, u32[]{:S(2)}) collective-permute-start(s16[272,128]{1,0:T(8,128)(2,1)S(1)} %get-tuple-element.23), channel_id=1, source_target_pairs={{0,2},{2,0},{1,3},{3,1},{4,6},{6,4},{5,7},{7,5},{8,10},{10,8},{9,1... | collective-permute-start | bytes 208904 | tf_op jit(solution)/shard_map/ppermute | solution.py:428
  25.4 3.2 %collective-permute-start.2 = (f32[256,128]{1,0:T(8,128)S(1)}, f32[256,128]{1,0:T(8,128)S(1)}, u32[]{:S(2)}, u32[]{:S(2)}) collective-permute-start(f32[256,128]{1,0:T(8,128)S(1)} %shard_map.107.half_ref), channel_id=1, source_target_pairs={{0,1},{1,0},{2,3},{3,2},{4,5},{5,4},{6,7},{7,6},{8,9},{9,8},{10,11... | collective-permute-start | bytes 393224 | tf_op jit(solution)/shard_map/ppermute | solution.py:430
  70.9 11.4 %collective-permute-start.3 = (s16[64,128]{1,0:T(8,128)(2,1)S(1)}, s16[64,128]{1,0:T(8,128)(2,1)S(1)}, u32[]{:S(2)}, u32[]{:S(2)}) collective-permute-start(s16[64,128]{1,0:T(8,128)(2,1)S(1)} %get-tuple-element.25), channel_id=1, source_target_pairs={{0,256},{4,260},{8,264},{12,268},{16,272},{20,276},{24,280},{28,28... | collective-permute-start | bytes 49160 | tf_op jit(solution)/shard_map/ppermute | solution.py:458

commit v8 on v7

--- a/solution.py
+++ b/solution.py
@@ -44,7 +44,7 @@
     return bounds
 
 
-CUT = 512
+CUT = 768
 
 
 def low_kernel(

time: 83.3 us -> 83.2 us (level)
  no operation moved by 1% of the time
where the time goes in v8:
time: 83.2 us; the launch traced here: 82.8 us
  blocking collectives  39.2 us (47%)
  starting transfers between devices  28.2 us (34%)
  Pallas kernels  8.09 us (10%)
  waiting for transfers between devices  6.63 us (8%)
    all_to_all x1, blocking collectives, shards(): lax.all_to_all(pieces, BOTH, 0, 0, tiled=True, axis_index_groups=first)  18.6 us
    ppermute x1, starting transfers between devices, shards(): far = lax.ppermute(packed, 'mp', far_pairs)  14.8 us
    all_to_all x1, blocking collectives, shards(): lax.all_to_all(pieces, BOTH, 0, 0, tiled=True, axis_index_groups=second)  12 us
    ppermute x1, starting transfers between devices, shards(): lax.ppermute(packed, 'dp', [(i, (i + count // 2) % count) for i in range(...  9.51 us
    all_to_all x1, blocking collectives, shards(): lax.all_to_all(pieces, BOTH, 0, 0, tiled=True, axis_index_groups=third)  8.65 us
    ppermute x1, waiting for transfers between devices, shards(): far = lax.ppermute(packed, 'mp', far_pairs)  4.16 us
    pallas_call x1, Pallas kernels, shards(): call(low_kernel, [((half, 128), F32), ((POLICIES, tokens), I32), (acts.sh...  2.38 us
    ppermute x1, starting transfers between devices, shards(): got = lax.ppermute(send, 'mp', core_pairs)  1.92 us
  transfers between devices with their start and end apart: 4, of which 4 were waited for; matrix products, arithmetic and copies ran while one was open for 0% of the time, Pallas kernels for 2%

profile of v8, /device:TPU:32, one launch (start us, length us, event | category | flops | bytes accessed | tf_op | source)
XLA Modules:
  0.0 82.8 jit_solution(8590783477359332574)
XLA Ops:
  0.6 2.4 %shard_map.104 = (f32[256,128]{1,0:T(8,128)S(1)}, s32[8,512]{1,0:T(8,128)S(1)}, bf16[512,1152]{1,0:T(8,128)(2,1)S(1)}, bf16[512,512]{1,0:T(8,128)(2,1)S(1)}, bf1...) custom-call(s32[1,8]{1,0:T(1,128)} %lengths_hbm.1, ...), custom_call_target="tpu_custom_call" | custom-call | tf_op jit(solution)/shard_map/pallas_call | solution.py:403
  3.0 1.9 %collective-permute-start = (f32[256,128]{1,0:T(8,128)S(1)}, f32[256,128]{1,0:T(8,128)S(1)}, u32[]{:S(2)}, u32[]{:S(2)}) collective-permute-start(f32[256,128]{1,0:T(8,128)S(1)} %get-tuple-element.21), channel_id=1, source_target_pairs={{0,1},{1,0},{2,3},{3,2},{4,5},{5,4},{6,7},{7,6},{8,9},{9,8},{10,11... | collective-permute-start | bytes 393224 | tf_op jit(solution)/shard_map/ppermute | solution.py:425
  4.9 0.8 shard_map.105.keep_ref
  5.7 0.5 collective-permute-done.got_ref
  6.3 0.1 shard_map.106
  6.3 14.8 %collective-permute-start.1 = (s16[272,128]{1,0:T(8,128)(2,1)S(1)}, s16[272,128]{1,0:T(8,128)(2,1)S(1)}, u32[]{:S(2)}, u32[]{:S(2)}) collective-permute-start(s16[272,128]{1,0:T(8,128)(2,1)S(1)} %get-tuple-element.23), channel_id=1, source_target_pairs={{0,2},{2,0},{1,3},{3,1},{4,6},{6,4},{5,7},{7,5},{8,10},{10,8},{9,1... | collective-permute-start | bytes 208904 | tf_op jit(solution)/shard_map/ppermute | solution.py:428
  21.2 4.2 %collective-permute-done.1.got_ref = s16[272,128]{1,0:T(8,128)(2,1)S(1)} collective-permute-done((s16[272,128]{1,0:T(8,128)(2,1)S(1)}, s16[272,128]{1,0:T(8,128)(2,1)S(1)}, u32[]{:S(2)}, u32[]{:S(2)}) %collective-permute-start.1) | collective-permute-done | bytes 69664 | tf_op jit(solution)/shard_map/ppermute | solution.py:428
  25.3 1.9 %collective-permute-start.2 = (f32[256,128]{1,0:T(8,128)S(1)}, f32[256,128]{1,0:T(8,128)S(1)}, u32[]{:S(2)}, u32[]{:S(2)}) collective-permute-start(f32[256,128]{1,0:T(8,128)S(1)} %shard_map.107.half_ref), channel_id=1, source_target_pairs={{0,1},{1,0},{2,3},{3,2},{4,5},{5,4},{6,7},{7,6},{8,9},{9,8},{10,11... | collective-permute-start | bytes 393224 | tf_op jit(solution)/shard_map/ppermute | solution.py:430
  27.3 1.2 %shard_map.108.sum_ref = f32[512,1664]{1,0:T(8,128)S(1)} custom-call(s32[8,512]{1,0:T(8,128)S(1)} %get-tuple-element.14.owner_ref, f32[256,128]{1,0:T(8,128)S(1)} %shard_map.107.half_ref, bf16[512,1152]{1,0:T(8,128)(2,1)S(1)} %get-tuple-element.15.acts_ref, bf16[512,512]{1,0:T(8,128)(2,1)S(1)} %get-tuple-element.16.cot_ref), custom_call_target="tpu_custom_call" | custom-call | tf_op jit(solution)/shard_map/pallas_call | solution.py:435
  28.5 0.1 collective-permute-done.2.half_ref
  28.6 1.8 %shard_map.109 = s16[4,1680,128]{2,1,0:T(8,128)(2,1)S(1)} custom-call(s32[8,512]{1,0:T(8,128)S(1)} %get-tuple-element.14.owner_ref, f32[256,128]{1,0:T(8,128)S(1)} %collective-permute-done.2.half_ref, bf16[512,1152]{1,0:T(8,128)(2,1)S(1)} %get-tuple-element.15.acts_ref, bf16[512,512]{1,0:T(8,128)(2,1)S(1)} %get-tuple-element.16.cot_ref, ...), custom_call_target="tpu_custom_call" | custom-call | tf_op jit(solution)/shard_map/pallas_call | solution.py:436
  30.4 18.6 %all_to_all.15.got_ref = s16[4,1680,128]{2,1,0:T(8,128)(2,1)S(1)} all-to-all(s16[4,1680,128]{2,1,0:T(8,128)(2,1)S(1)} %shard_map.109), channel_id=1, replica_groups={{0,16,32,48},{1,5,9,13},{4,20,36,52},{17,21,25,29},{8,24,40,56},{33,37,..., dimensions={0} | all-to-all | bytes 3440640 | tf_op jit(solution)/shard_map/all_to_all | solution.py:442
  49.0 0.8 shard_map.110
  49.8 12.0 %all_to_all.16.got_ref = s16[4,32,1792]{2,1,0:T(8,128)(2,1)S(1)} all-to-all(s16[4,32,1792]{2,1,0:T(8,128)(2,1)S(1)} %shard_map.110), channel_id=1, replica_groups={{0,4,8,12},{1,17,33,49},{16,20,24,28},{5,21,37,53},{32,36,40,44},{9,25,..., dimensions={0} | all-to-all | bytes 917504 | tf_op jit(solution)/shard_map/all_to_all | solution.py:446
  61.8 0.3 shard_map.111
  62.1 8.6 %all_to_all.17.got_ref = s16[4,112,128]{2,1,0:T(8,128)(2,1)S(1)} all-to-all(s16[4,112,128]{2,1,0:T(8,128)(2,1)S(1)} %shard_map.111), channel_id=1, replica_groups={{0,64,128,192},{1,65,129,193},{2,66,130,194},{3,67,131,195},{4,68,132,1..., dimensions={0} | all-to-all | bytes 229376 | tf_op jit(solution)/shard_map/all_to_all | solution.py:451
  70.7 0.1 shard_map.112
  70.9 9.5 %collective-permute-start.3 = (s16[64,128]{1,0:T(8,128)(2,1)S(1)}, s16[64,128]{1,0:T(8,128)(2,1)S(1)}, u32[]{:S(2)}, u32[]{:S(2)}) collective-permute-start(s16[64,128]{1,0:T(8,128)(2,1)S(1)} %get-tuple-element.25), channel_id=1, source_target_pairs={{0,256},{4,260},{8,264},{12,268},{16,272},{20,276},{24,280},{28,28... | collective-permute-start | bytes 49160 | tf_op jit(solution)/shard_map/ppermute | solution.py:458
  80.4 1.8 %collective-permute-done.3.got_ref = s16[64,128]{1,0:T(8,128)(2,1)S(1)} collective-permute-done((s16[64,128]{1,0:T(8,128)(2,1)S(1)}, s16[64,128]{1,0:T(8,128)(2,1)S(1)}, u32[]{:S(2)}, u32[]{:S(2)}) %collective-permute-start.3) | collective-permute-done | bytes 16416 | tf_op jit(solution)/shard_map/ppermute | solution.py:458
  82.2 0.6 shard_map.113
  (1 shorter events, 0.0 us)
Async XLA Ops:
  3.0 3.2 %collective-permute-start = (f32[256,128]{1,0:T(8,128)S(1)}, f32[256,128]{1,0:T(8,128)S(1)}, u32[]{:S(2)}, u32[]{:S(2)}) collective-permute-start(f32[256,128]{1,0:T(8,128)S(1)} %get-tuple-element.21), channel_id=1, source_target_pairs={{0,1},{1,0},{2,3},{3,2},{4,5},{5,4},{6,7},{7,6},{8,9},{9,8},{10,11... | collective-permute-start | bytes 393224 | tf_op jit(solution)/shard_map/ppermute | solution.py:425
  6.3 19.0 %collective-permute-start.1 = (s16[272,128]{1,0:T(8,128)(2,1)S(1)}, s16[272,128]{1,0:T(8,128)(2,1)S(1)}, u32[]{:S(2)}, u32[]{:S(2)}) collective-permute-start(s16[272,128]{1,0:T(8,128)(2,1)S(1)} %get-tuple-element.23), channel_id=1, source_target_pairs={{0,2},{2,0},{1,3},{3,1},{4,6},{6,4},{5,7},{7,5},{8,10},{10,8},{9,1... | collective-permute-start | bytes 208904 | tf_op jit(solution)/shard_map/ppermute | solution.py:428
  25.3 3.2 %collective-permute-start.2 = (f32[256,128]{1,0:T(8,128)S(1)}, f32[256,128]{1,0:T(8,128)S(1)}, u32[]{:S(2)}, u32[]{:S(2)}) collective-permute-start(f32[256,128]{1,0:T(8,128)S(1)} %shard_map.107.half_ref), channel_id=1, source_target_pairs={{0,1},{1,0},{2,3},{3,2},{4,5},{5,4},{6,7},{7,6},{8,9},{9,8},{10,11... | collective-permute-start | bytes 393224 | tf_op jit(solution)/shard_map/ppermute | solution.py:430
  70.9 11.4 %collective-permute-start.3 = (s16[64,128]{1,0:T(8,128)(2,1)S(1)}, s16[64,128]{1,0:T(8,128)(2,1)S(1)}, u32[]{:S(2)}, u32[]{:S(2)}) collective-permute-start(s16[64,128]{1,0:T(8,128)(2,1)S(1)} %get-tuple-element.25), channel_id=1, source_target_pairs={{0,256},{4,260},{8,264},{12,268},{16,272},{20,276},{24,280},{28,28... | collective-permute-start | bytes 49160 | tf_op jit(solution)/shard_map/ppermute | solution.py:458
